TPU v7x, 128 devices: a whole 4x4x4 slice. The times are simulated.
128 devices in a mesh: fsdp: 64 (over x, y_hi, z, core), rep: 2 (over y_lo).
Axes of the slice: x: 4, y: 4 (y_hi: 2, y_lo: 2; y = y_hi * 2 + y_lo), z: 4, core: 2. Of those that a mesh axis runs over, the one named last changes fastest.
Arguments:
- tokens: bfloat16 [2, 16384, 1152], P(None, ('fsdp', 'rep')), may hold values from -6 to 6
- picture: int32 [2, 16384], replicated, may hold values from -16384 to 319, as said below
- cotangent: bfloat16 [2, 16384, 1152], P(None, ('fsdp', 'rep')), may hold values from -6 to 6
- ln1_gain: float32 [1152], replicated, may hold values from 0.1 to 1.9
- ln1_bias: float32 [1152], replicated, may hold values from -1.75 to 1.75
- w_query: bfloat16 [1152, 1152], P('fsdp'), may hold values from -0.1875 to 0.1875
- b_query: float32 [1152], replicated, may hold values from -1.75 to 1.75
- w_key: bfloat16 [1152, 1152], P('fsdp'), may hold values from -0.1875 to 0.1875
- w_value: bfloat16 [1152, 1152], P('fsdp'), may hold values from -0.1875 to 0.1875
- b_value: float32 [1152], replicated, may hold values from -1.75 to 1.75
- w_out: bfloat16 [1152, 1152], P('fsdp'), may hold values from -0.875 to 0.875
- b_out: float32 [1152], replicated, may hold values from -1.75 to 1.75
- ln2_gain: float32 [1152], replicated, may hold values from 0.1 to 1.9
- ln2_bias: float32 [1152], replicated, may hold values from -1.75 to 1.75
- w_fc1: bfloat16 [1152, 4304], P('fsdp'), may hold values from -0.1875 to 0.1875
- b_fc1: float32 [4304], replicated, may hold values from -1.75 to 1.75
- w_fc2: bfloat16 [4304, 1152], P(None, 'fsdp'), may hold values from -0.09375 to 0.09375
- b_fc2: float32 [1152], replicated, may hold values from -1.75 to 1.75
Outputs:
- mixed: bfloat16 [2, 16384, 1152], P(None, ('fsdp', 'rep'))
- grad_tokens: bfloat16 [2, 16384, 1152], P(None, ('fsdp', 'rep'))
- grad_ln1_gain: float32 [1152], replicated
- grad_ln1_bias: float32 [1152], replicated
- grad_w_query: float32 [1152, 1152], P('fsdp')
- grad_b_query: float32 [1152], replicated
- grad_w_key: float32 [1152, 1152], P('fsdp')
- grad_w_value: float32 [1152, 1152], P('fsdp')
- grad_b_value: float32 [1152], replicated
- grad_w_out: float32 [1152, 1152], P('fsdp')
- grad_b_out: float32 [1152], replicated
- grad_ln2_gain: float32 [1152], replicated
- grad_ln2_bias: float32 [1152], replicated
- grad_w_fc1: float32 [1152, 4304], P('fsdp')
- grad_b_fc1: float32 [4304], replicated
- grad_w_fc2: float32 [4304, 1152], P(None, 'fsdp')
- grad_b_fc2: float32 [1152], replicated
Inputs may be any that keep to these rules, and one draw needn't show every extreme that they name: Tokens with one nonnegative id form one picture of 100 to 1024 consecutive tokens inside one packed row of 2048 tokens (rows are consecutive runs of 2048 tokens); each row begins with a picture of odd length followed by a picture of exactly 1024 tokens; every negative id marks a padding token and occurs once in its micro-batch.
All inputs are finite; a program needn't handle non-finite values.
Results may differ from a plain program's by a relative error of at most 0.014.
Values may be sent and summed in bfloat16 or wider, within the bound.
A program may use at most 320 MiB of HBM per device.

v0:
```python
import jax
import jax.numpy as jnp
from jax import lax
from jax.sharding import PartitionSpec as P

D = 1152
HEADS = 16
HEAD_DIM = 72
FF = 4304
PIC_MAX = 1024


EPS = 1e-06
NEG = -1e30


def passed_along(value, axis, steps):
    count = lax.axis_size(axis)
    first, last = (max(0, -steps), min(count, count - steps))
    return lax.ppermute(value, axis, [(source, source + steps) for source in range(first, last)])


def normalize(values, gain, bias):
    center = values - jnp.mean(values, axis=-1, keepdims=True)
    spread = jnp.mean(center * center, axis=-1, keepdims=True)
    return center * lax.rsqrt(spread + EPS) * gain + bias


def gelu_tanh(values):
    return jax.nn.gelu(values, approximate=True)


def matmul(left, right):
    return jnp.dot(left, right, preferred_element_type=jnp.float32)


def left_times(left, right):
    return lax.dot_general(
        left, right, (((0,), (0,)), ((), ())), preferred_element_type=jnp.float32
    )


def right_times(left, right):
    return lax.dot_general(
        left, right, (((1,), (1,)), ((), ())), preferred_element_type=jnp.float32
    )


def column_sum(values):
    return jnp.sum(values.astype(jnp.float32), axis=0)


def body(
    tokens,
    picture,
    cotangent,
    ln1_gain,
    ln1_bias,
    w_query,
    b_query,
    w_key,
    w_value,
    b_value,
    w_out,
    b_out,
    ln2_gain,
    ln2_bias,
    w_fc1,
    b_fc1,
    w_fc2,
    b_fc2,
):
    micro, count, width_model = tokens.shape
    reach = (count + PIC_MAX - 2) // count
    window_len = (2 * reach + 1) * count
    total = picture.shape[1]
    location = lax.axis_index(("fsdp", "rep"))
    scale = HEAD_DIM ** (-0.5)
    shards = (w_query, w_key, w_value, w_out, w_fc1, w_fc2)
    full_shapes = ((D, D), (D, D), (D, D), (D, D), (D, FF), (FF, D))
    mat_sums = tuple((jnp.zeros(shape, jnp.float32) for shape in full_shapes))
    vec_sums = tuple(
        (
            jnp.zeros(item.shape, jnp.float32)
            for item in (
                ln1_gain,
                ln1_bias,
                b_query,
                b_value,
                b_out,
                ln2_gain,
                ln2_bias,
                b_fc1,
                b_fc2,
            )
        )
    )
    results = []
    grad_list = []
    for batch in range(micro):
        weights = (
            lax.all_gather(shards[0], "fsdp", axis=0, tiled=True),
            lax.all_gather(shards[1], "fsdp", axis=0, tiled=True),
            lax.all_gather(shards[2], "fsdp", axis=0, tiled=True),
            lax.all_gather(shards[3], "fsdp", axis=0, tiled=True),
            lax.all_gather(shards[4], "fsdp", axis=0, tiled=True),
            lax.all_gather(shards[5], "fsdp", axis=1, tiled=True),
        )
        full_query, full_key, full_value, full_out, full_up, full_down = weights
        ids = picture[batch]
        filler = jnp.full((reach * count,), -total - 1, jnp.int32)
        padded_ids = jnp.concatenate([filler, ids, filler])
        window = lax.dynamic_slice_in_dim(padded_ids, location * count, window_len)
        mine = lax.dynamic_slice_in_dim(ids, location * count, count)
        allowed = (mine[:, None] == window[None, :])[None]
        inputs = tokens[batch].astype(jnp.float32)
        normed1 = normalize(inputs, ln1_gain, ln1_bias).astype(jnp.bfloat16)
        query = (matmul(normed1, full_query) + b_query).astype(jnp.bfloat16)
        key_rows = matmul(normed1, full_key).astype(jnp.bfloat16)
        value_rows = (matmul(normed1, full_value) + b_value).astype(jnp.bfloat16)
        key_parts = []
        value_parts = []
        for offset in range(-reach, reach + 1):
            if offset == 0:
                key_parts.append(key_rows)
                value_parts.append(value_rows)
            else:
                far_key, far_value = passed_along((key_rows, value_rows), ("fsdp", "rep"), -offset)
                key_parts.append(far_key)
                value_parts.append(far_value)
        keys_heads = jnp.concatenate(key_parts, axis=0).reshape(window_len, HEADS, HEAD_DIM)
        values_heads = jnp.concatenate(value_parts, axis=0).reshape(window_len, HEADS, HEAD_DIM)
        query_heads = query.reshape(count, HEADS, HEAD_DIM)
        scores = (
            jnp.einsum("qhd,khd->hqk", query_heads, keys_heads, preferred_element_type=jnp.float32)
            * scale
        )
        scores = jnp.where(allowed, scores, NEG)
        top = jnp.max(scores, axis=-1, keepdims=True)
        expo = jnp.exp(scores - top)
        mass = jnp.sum(expo, axis=-1, keepdims=True)
        probs = expo / mass
        logsum = top + jnp.log(mass)
        attended = jnp.einsum(
            "hqk,khd->qhd",
            probs.astype(jnp.bfloat16),
            values_heads,
            preferred_element_type=jnp.float32,
        )
        attended = attended.reshape(count, D).astype(jnp.bfloat16)
        mid = inputs + matmul(attended, full_out) + b_out
        normed2 = normalize(mid, ln2_gain, ln2_bias).astype(jnp.bfloat16)
        hidden_pre = matmul(normed2, full_up) + b_fc1
        active = gelu_tanh(hidden_pre).astype(jnp.bfloat16)
        result = mid + matmul(active, full_down) + b_fc2
        results.append(result.astype(jnp.bfloat16))
        weights = (
            lax.all_gather(shards[0], "fsdp", axis=0, tiled=True),
            lax.all_gather(shards[1], "fsdp", axis=0, tiled=True),
            lax.all_gather(shards[2], "fsdp", axis=0, tiled=True),
            lax.all_gather(shards[3], "fsdp", axis=0, tiled=True),
            lax.all_gather(shards[4], "fsdp", axis=0, tiled=True),
            lax.all_gather(shards[5], "fsdp", axis=1, tiled=True),
        )
        full_query, full_key, full_value, full_out, full_up, full_down = weights
        grad_out = cotangent[batch].astype(jnp.float32)
        grad_branch = grad_out.astype(jnp.bfloat16)
        grad_down = left_times(active, grad_branch)
        grad_bias_down = column_sum(grad_branch)
        grad_active = right_times(grad_branch, full_down)
        gelu_value, gelu_back = jax.vjp(gelu_tanh, hidden_pre)
        grad_hidden = gelu_back(grad_active)[0].astype(jnp.bfloat16)
        grad_up = left_times(normed2, grad_hidden)
        grad_bias_up = column_sum(grad_hidden)
        grad_normed2 = right_times(grad_hidden, full_up)
        norm_value, norm2_back = jax.vjp(normalize, mid, ln2_gain, ln2_bias)
        grad_mid_norm, grad_gain_two, grad_bias_two = norm2_back(grad_normed2)
        grad_mid = grad_out + grad_mid_norm
        grad_attn_out = grad_mid.astype(jnp.bfloat16)
        grad_outproj = left_times(attended, grad_attn_out)
        grad_bias_out = column_sum(grad_attn_out)
        grad_attended = (
            right_times(grad_attn_out, full_out)
            .astype(jnp.bfloat16)
            .reshape(count, HEADS, HEAD_DIM)
        )
        scores = (
            jnp.einsum("qhd,khd->hqk", query_heads, keys_heads, preferred_element_type=jnp.float32)
            * scale
        )
        scores = jnp.where(allowed, scores, NEG)
        probs_again = jnp.where(allowed, jnp.exp(scores - logsum), 0.0)
        grad_probs = jnp.einsum(
            "qhd,khd->hqk", grad_attended, values_heads, preferred_element_type=jnp.float32
        )
        rowdot = jnp.sum(probs_again * grad_probs, axis=-1, keepdims=True)
        grad_scores = (probs_again * (grad_probs - rowdot)).astype(jnp.bfloat16)
        grad_query = (
            jnp.einsum("hqk,khd->qhd", grad_scores, keys_heads, preferred_element_type=jnp.float32)
            * scale
        ).reshape(count, D)
        grad_keys = (
            jnp.einsum("hqk,qhd->khd", grad_scores, query_heads, preferred_element_type=jnp.float32)
            * scale
        ).reshape(window_len, D)
        grad_values = jnp.einsum(
            "hqk,qhd->khd",
            probs_again.astype(jnp.bfloat16),
            grad_attended,
            preferred_element_type=jnp.float32,
        ).reshape(window_len, D)
        key_total = grad_keys[reach * count : (reach + 1) * count]
        value_total = grad_values[reach * count : (reach + 1) * count]
        for offset in range(-reach, reach + 1):
            if offset != 0:
                begin = (offset + reach) * count
                back_key, back_value = (
                    passed_along(
                        grad_keys[begin : begin + count].astype(jnp.bfloat16),
                        ("fsdp", "rep"),
                        offset,
                    ).astype(jnp.float32),
                    passed_along(
                        grad_values[begin : begin + count].astype(jnp.bfloat16),
                        ("fsdp", "rep"),
                        offset,
                    ).astype(jnp.float32),
                )
                key_total = key_total + back_key
                value_total = value_total + back_value
        grad_query_low = grad_query.astype(jnp.bfloat16)
        grad_key_low = key_total.astype(jnp.bfloat16)
        grad_value_low = value_total.astype(jnp.bfloat16)
        grad_wq = left_times(normed1, grad_query_low)
        grad_wk = left_times(normed1, grad_key_low)
        grad_wv = left_times(normed1, grad_value_low)
        grad_normed1 = (
            right_times(grad_query_low, full_query)
            + right_times(grad_key_low, full_key)
            + right_times(grad_value_low, full_value)
        )
        norm_first, norm1_back = jax.vjp(normalize, inputs, ln1_gain, ln1_bias)
        grad_in_norm, grad_gain_one, grad_bias_one = norm1_back(grad_normed1)
        grad_list.append((grad_mid + grad_in_norm).astype(jnp.bfloat16))
        mat_terms = (grad_wq, grad_wk, grad_wv, grad_outproj, grad_up, grad_down)
        mat_sums = tuple((left + right for left, right in zip(mat_sums, mat_terms)))
        vec_terms = (
            grad_gain_one,
            grad_bias_one,
            column_sum(grad_query_low),
            column_sum(grad_value_low),
            grad_bias_out,
            grad_gain_two,
            grad_bias_two,
            grad_bias_up,
            grad_bias_down,
        )
        vec_sums = tuple((left + right for left, right in zip(vec_sums, vec_terms)))
    shares = (
        lax.psum_scatter(mat_sums[0], ("fsdp", "rep"), scatter_dimension=0, tiled=True),
        lax.psum_scatter(mat_sums[1], ("fsdp", "rep"), scatter_dimension=0, tiled=True),
        lax.psum_scatter(mat_sums[2], ("fsdp", "rep"), scatter_dimension=0, tiled=True),
        lax.psum_scatter(mat_sums[3], ("fsdp", "rep"), scatter_dimension=0, tiled=True),
        lax.psum_scatter(mat_sums[4], ("fsdp", "rep"), scatter_dimension=0, tiled=True),
        lax.psum_scatter(mat_sums[5], ("fsdp", "rep"), scatter_dimension=1, tiled=True),
    )
    owned = (
        lax.all_gather(shares[0].astype(jnp.bfloat16), "rep", axis=0, tiled=True).astype(
            jnp.float32
        ),
        lax.all_gather(shares[1].astype(jnp.bfloat16), "rep", axis=0, tiled=True).astype(
            jnp.float32
        ),
        lax.all_gather(shares[2].astype(jnp.bfloat16), "rep", axis=0, tiled=True).astype(
            jnp.float32
        ),
        lax.all_gather(shares[3].astype(jnp.bfloat16), "rep", axis=0, tiled=True).astype(
            jnp.float32
        ),
        lax.all_gather(shares[4].astype(jnp.bfloat16), "rep", axis=0, tiled=True).astype(
            jnp.float32
        ),
        lax.all_gather(shares[5].astype(jnp.bfloat16), "rep", axis=1, tiled=True).astype(
            jnp.float32
        ),
    )
    vectors = lax.psum(vec_sums, ("fsdp", "rep"))
    mixed = jnp.stack(results, axis=0)
    grad_tokens = jnp.stack(grad_list, axis=0)
    return (
        mixed,
        grad_tokens,
        vectors[0],
        vectors[1],
        owned[0],
        vectors[2],
        owned[1],
        owned[2],
        vectors[3],
        owned[3],
        vectors[4],
        vectors[5],
        vectors[6],
        owned[4],
        vectors[7],
        owned[5],
        vectors[8],
    )


def solution(mesh):
    placed = (
        P(None, ("fsdp", "rep"), None),
        P(),
        P(None, ("fsdp", "rep"), None),
        P(),
        P(),
        P("fsdp", None),
        P(),
        P("fsdp", None),
        P("fsdp", None),
        P(),
        P("fsdp", None),
        P(),
        P(),
        P(),
        P("fsdp", None),
        P(),
        P(None, "fsdp"),
        P(),
    )
    return jax.shard_map(
        body,
        mesh=mesh,
        in_specs=placed,
        out_specs=(
            P(None, ("fsdp", "rep"), None),
            P(None, ("fsdp", "rep"), None),
            P(),
            P(),
            P("fsdp", None),
            P(),
            P("fsdp", None),
            P("fsdp", None),
            P(),
            P("fsdp", None),
            P(),
            P(),
            P(),
            P("fsdp", None),
            P(),
            P(None, "fsdp"),
            P(),
        ),
        check_vma=False,
    )
```

profile of v0, /device:TPU:0, one launch (start us, length us, event | category | flops | bytes accessed | tf_op | source)
XLA Modules:
  0.0 1929.9 jit_solution(362810375310519763)
XLA Ops:
  16.8 67.6 %all-gather.19.cloned.1.call-done = bf16[64,18,1152]{2,1,0:T(8,128)(2,1)} async-done(((bf16[1,18,1152]{2,1,0:T(8,128)(2,1)}), bf16[64,18,1152]{2,1,0:T(8,128)(2,1)}) %all-gather.19.cloned.1.call-update) | async-done | bytes 2654224 | tf_op jit(solution)/shard_map/all_gather | solution.py:104
  108.8 72.4 %all-gather.21.cloned.1.call-done = bf16[64,18,1152]{2,1,0:T(8,128)(2,1)} async-done(((bf16[1,18,1152]{2,1,0:T(8,128)(2,1)}), bf16[64,18,1152]{2,1,0:T(8,128)(2,1)}) %all-gather.21.cloned.1.call-update) | async-done | bytes 2654224 | tf_op jit(solution)/shard_map/all_gather | solution.py:102
  192.9 59.0 %all-gather.23.cloned.1.call-done = bf16[64,18,1152]{2,1,0:T(8,128)(2,1)} async-done(((bf16[1,18,1152]{2,1,0:T(8,128)(2,1)}), bf16[64,18,1152]{2,1,0:T(8,128)(2,1)}) %all-gather.23.cloned.1.call-update) | async-done | bytes 2654224 | tf_op jit(solution)/shard_map/all_gather | solution.py:103
  262.5 59.9 %all-gather.25.cloned.1.call-done = bf16[64,18,1152]{2,1,0:T(8,128)(2,1)} async-done(((bf16[1,18,1152]{2,1,0:T(8,128)(2,1)}), bf16[64,18,1152]{2,1,0:T(8,128)(2,1)}) %all-gather.25.cloned.1.call-update) | async-done | bytes 2654224 | tf_op jit(solution)/shard_map/all_gather | solution.py:105
  358.4 12.8 collective-permute-start.50
  447.8 20.0 %collective-permute-start.4 = (bf16[128,1152]{1,0:T(8,128)(2,1)S(1)}, bf16[128,1152]{1,0:T(8,128)(2,1)S(1)}, u32[]{:S(2)}, u32[]{:S(2)}) collective-permute-start(bf16[128,1152]{1,0:T(8,128)(2,1)S(1)} %copy-done.123), channel_id=1, source_target_pairs={{0,4},{1,5},{2,6},{3,7},{4,8},{5,9},{6,10},{7,11},{8,12},{9,13},{1... | collective-permute-start | bytes 884744 | tf_op jit(solution)/shard_map/ppermute | solution.py:20
  483.9 15.4 collective-permute-start.16
  609.7 21.0 %collective-permute-done.60 = bf16[128,1152]{1,0:T(8,128)(2,1)S(1)} collective-permute-done((bf16[128,1152]{1,0:T(8,128)(2,1)S(1)}, bf16[128,1152]{1,0:T(8,128)(2,1)S(1)}, u32[]{:S(2)}, u32[]{:S(2)}) %collective-permute-start.60) | collective-permute-done | bytes 294944 | tf_op jit(solution)/shard_map/ppermute | solution.py:20
  633.3 17.7 collective-permute-done.62
  653.7 30.9 %collective-permute-done.8 = bf16[128,1152]{1,0:T(8,128)(2,1)S(1)} collective-permute-done((bf16[128,1152]{1,0:T(8,128)(2,1)S(1)}, bf16[128,1152]{1,0:T(8,128)(2,1)S(1)}, u32[]{:S(2)}, u32[]{:S(2)}) %collective-permute-start.8) | collective-permute-done | bytes 294944 | tf_op jit(solution)/shard_map/ppermute | solution.py:20
  715.8 13.0 collective-permute-done.27
  729.6 17.5 collective-permute-done.28
  785.7 12.2 fusion.3
  852.3 15.7 reshape.489
  882.9 15.7 reshape.491
  948.6 15.0 multiply_reduce_fusion
  963.6 13.1 multiply_convert_fusion
  989.4 12.4 fusion.231
  1004.5 14.3 multiply_reduce_fusion.1
  1018.8 13.1 multiply_convert_fusion.1
  1041.4 12.4 fusion.229
  1103.5 25.0 %collective-permute-start.108 = (bf16[128,1152]{0,1:T(8,128)(2,1)}, bf16[128,1152]{0,1:T(8,128)(2,1)}, u32[]{:S(2)}, u32[]{:S(2)}) collective-permute-start(bf16[128,1152]{0,1:T(8,128)(2,1)} %bitcast.84), channel_id=1, source_target_pairs={{0,5},{1,6},{2,7},{3,8},{4,9},{5,10},{6,11},{7,12},{8,13},{9,14},{... | collective-permute-start | bytes 884744 | tf_op jit(solution)/shard_map/ppermute | solution.py:20
  1134.3 12.9 convolution_add_fusion.1
  1147.2 12.8 convolution_add_fusion
  1220.5 15.9 collective-permute-done.98
  1300.3 12.0 collective-permute-done.116
  1312.4 14.0 collective-permute-start.79
  1362.3 13.0 collective-permute-start.72
  1396.8 15.9 collective-permute-done.68
  1414.0 16.8 collective-permute-start.94
  1491.0 13.0 collective-permute-done.84
  1528.0 345.7 %all-reduce.8 = (f32[1152]{0:T(1024)}, f32[1152]{0:T(1024)}, bf16[1152,1152]{1,0:T(8,128)(2,1)}, f32[1152]{0:T(1024)}, bf16[1152,1152]{1,0:T(8,128)(2,1)}, /*ind...) all-reduce(f32[1152]{0:T(1024)} %add.611, ...), channel_id=1, replica_groups=mesh['fsdp'=64,'rep'=2] {'fsdp','rep'}, use_global_device_ids=true, to_apply=%region_24.25 | all-reduce | flops 15238352 | bytes 91457152 | tf_op jit(solution)/shard_map/psum | solution.py:287
  (840 shorter events, 882.9 us)
Async XLA Ops:
  7.2 77.2 %all-gather.19.cloned.1.call-start = ((), (), s32[]{:S(2)}) async-start(), calls=%async_computation | async-start | bytes 3594240 | tf_op jit(solution)/shard_map/all_gather | solution.py:104
  8.0 173.3 %all-gather.21.cloned.1.call-start = ((), (), s32[]{:S(2)}) async-start(), calls=%async_computation.1 | async-start | bytes 3594240 | tf_op jit(solution)/shard_map/all_gather | solution.py:102
  8.7 243.2 %all-gather.23.cloned.1.call-start = ((), (), s32[]{:S(2)}) async-start(), calls=%async_computation.2 | async-start | bytes 3594240 | tf_op jit(solution)/shard_map/all_gather | solution.py:103
  9.4 313.0 %all-gather.25.cloned.1.call-start = ((), (), s32[]{:S(2)}) async-start(), calls=%async_computation.3 | async-start | bytes 3594240 | tf_op jit(solution)/shard_map/all_gather | solution.py:105
  10.0 842.2 %all-gather.27.cloned.1.call-start = ((), (), s32[]{:S(2)}) async-start(), calls=%async_computation.4 | async-start | bytes 13578240 | tf_op jit(solution)/shard_map/all_gather | solution.py:106
  10.6 872.3 %all-gather.29.cloned.1.call-start = ((), (), s32[]{:S(2)}) async-start(), calls=%async_computation.5 | async-start | bytes 13578240 | tf_op jit(solution)/shard_map/all_gather | solution.py:107
  90.4 235.9 %collective-permute-start.32 = (bf16[128,1152]{1,0:T(8,128)(2,1)}, bf16[128,1152]{1,0:T(8,128)(2,1)}, u32[]{:S(2)}, u32[]{:S(2)}) collective-permute-start(bf16[128,1152]{1,0:T(8,128)(2,1)} %fusion.24), channel_id=1, source_target_pairs={{0,8},{1,9},{2,10},{3,11},{4,12},{5,13},{6,14},{7,15},{8,16},{9,17... | collective-permute-start | bytes 884744 | tf_op jit(solution)/shard_map/ppermute | solution.py:20
  94.5 235.4 %collective-permute-start.33 = (bf16[128,1152]{1,0:T(8,128)(2,1)}, bf16[128,1152]{1,0:T(8,128)(2,1)}, u32[]{:S(2)}, u32[]{:S(2)}) collective-permute-start(bf16[128,1152]{1,0:T(8,128)(2,1)} %fusion.24), channel_id=1, source_target_pairs={{0,7},{1,8},{2,9},{3,10},{4,11},{5,12},{6,13},{7,14},{8,15},{9,16}... | collective-permute-start | bytes 884744 | tf_op jit(solution)/shard_map/ppermute | solution.py:20
  97.0 235.7 %collective-permute-start.34 = (bf16[128,1152]{1,0:T(8,128)(2,1)}, bf16[128,1152]{1,0:T(8,128)(2,1)}, u32[]{:S(2)}, u32[]{:S(2)}) collective-permute-start(bf16[128,1152]{1,0:T(8,128)(2,1)} %fusion.24), channel_id=1, source_target_pairs={{0,6},{1,7},{2,8},{3,9},{4,10},{5,11},{6,12},{7,13},{8,14},{9,15},... | collective-permute-start | bytes 884744 | tf_op jit(solution)/shard_map/ppermute | solution.py:20
  101.8 235.0 %collective-permute-start.35 = (bf16[128,1152]{1,0:T(8,128)(2,1)}, bf16[128,1152]{1,0:T(8,128)(2,1)}, u32[]{:S(2)}, u32[]{:S(2)}) collective-permute-start(bf16[128,1152]{1,0:T(8,128)(2,1)} %fusion.24), channel_id=1, source_target_pairs={{0,5},{1,6},{2,7},{3,8},{4,9},{5,10},{6,11},{7,12},{8,13},{9,14},{... | collective-permute-start | bytes 884744 | tf_op jit(solution)/shard_map/ppermute | solution.py:20
  104.1 235.1 %collective-permute-start.36 = (bf16[128,1152]{1,0:T(8,128)(2,1)}, bf16[128,1152]{1,0:T(8,128)(2,1)}, u32[]{:S(2)}, u32[]{:S(2)}) collective-permute-start(bf16[128,1152]{1,0:T(8,128)(2,1)} %fusion.24), channel_id=1, source_target_pairs={{0,4},{1,5},{2,6},{3,7},{4,8},{5,9},{6,10},{7,11},{8,12},{9,13},{1... | collective-permute-start | bytes 884744 | tf_op jit(solution)/shard_map/ppermute | solution.py:20
  336.9 223.0 %collective-permute-start.40 = (bf16[128,1152]{1,0:T(8,128)(2,1)}, bf16[128,1152]{1,0:T(8,128)(2,1)S(1)}, u32[]{:S(2)}, u32[]{:S(2)}) collective-permute-start(bf16[128,1152]{1,0:T(8,128)(2,1)} %fusion.24), channel_id=1, source_target_pairs={{1,0},{2,1},{3,2},{4,3},{5,4},{6,5},{7,6},{8,7},{9,8},{10,9},{11,1... | collective-permute-start | bytes 884744 | tf_op jit(solution)/shard_map/ppermute | solution.py:20
  339.2 222.0 %collective-permute-start.41 = (bf16[128,1152]{1,0:T(8,128)(2,1)}, bf16[128,1152]{1,0:T(8,128)(2,1)S(1)}, u32[]{:S(2)}, u32[]{:S(2)}) collective-permute-start(bf16[128,1152]{1,0:T(8,128)(2,1)} %fusion.24), channel_id=1, source_target_pairs={{2,0},{3,1},{4,2},{5,3},{6,4},{7,5},{8,6},{9,7},{10,8},{11,9},{12,... | collective-permute-start | bytes 884744 | tf_op jit(solution)/shard_map/ppermute | solution.py:20
  341.5 221.1 %collective-permute-start.42 = (bf16[128,1152]{1,0:T(8,128)(2,1)}, bf16[128,1152]{1,0:T(8,128)(2,1)S(1)}, u32[]{:S(2)}, u32[]{:S(2)}) collective-permute-start(bf16[128,1152]{1,0:T(8,128)(2,1)} %fusion.24), channel_id=1, source_target_pairs={{3,0},{4,1},{5,2},{6,3},{7,4},{8,5},{9,6},{10,7},{11,8},{12,9},{13... | collective-permute-start | bytes 884744 | tf_op jit(solution)/shard_map/ppermute | solution.py:20
  586.1 44.5 %collective-permute-start.60 = (bf16[128,1152]{1,0:T(8,128)(2,1)S(1)}, bf16[128,1152]{1,0:T(8,128)(2,1)S(1)}, u32[]{:S(2)}, u32[]{:S(2)}) collective-permute-start(bf16[128,1152]{1,0:T(8,128)(2,1)S(1)} %copy-done.124), channel_id=1, source_target_pairs={{5,0},{6,1},{7,2},{8,3},{9,4},{10,5},{11,6},{12,7},{13,8},{14,9},{... | collective-permute-start | bytes 884744 | tf_op jit(solution)/shard_map/ppermute | solution.py:20
  588.8 62.2 %collective-permute-start.62 = (bf16[128,1152]{1,0:T(8,128)(2,1)S(1)}, bf16[128,1152]{1,0:T(8,128)(2,1)S(1)}, u32[]{:S(2)}, u32[]{:S(2)}) collective-permute-start(bf16[128,1152]{1,0:T(8,128)(2,1)S(1)} %copy-done.124), channel_id=1, source_target_pairs={{7,0},{8,1},{9,2},{10,3},{11,4},{12,5},{13,6},{14,7},{15,8},{16,9}... | collective-permute-start | bytes 884744 | tf_op jit(solution)/shard_map/ppermute | solution.py:20
  597.1 55.2 %collective-permute-start.63 = (bf16[128,1152]{1,0:T(8,128)(2,1)S(1)}, bf16[128,1152]{1,0:T(8,128)(2,1)S(1)}, u32[]{:S(2)}, u32[]{:S(2)}) collective-permute-start(bf16[128,1152]{1,0:T(8,128)(2,1)S(1)} %copy-done.124), channel_id=1, source_target_pairs={{8,0},{9,1},{10,2},{11,3},{12,4},{13,5},{14,6},{15,7},{16,8},{17,9... | collective-permute-start | bytes 884744 | tf_op jit(solution)/shard_map/ppermute | solution.py:20
  608.2 76.5 %collective-permute-start.8 = (bf16[128,1152]{1,0:T(8,128)(2,1)S(1)}, bf16[128,1152]{1,0:T(8,128)(2,1)S(1)}, u32[]{:S(2)}, u32[]{:S(2)}) collective-permute-start(bf16[128,1152]{1,0:T(8,128)(2,1)S(1)} %copy-done.123), channel_id=1, source_target_pairs={{1,0},{2,1},{3,2},{4,3},{5,4},{6,5},{7,6},{8,7},{9,8},{10,9},{11,1... | collective-permute-start | bytes 884744 | tf_op jit(solution)/shard_map/ppermute | solution.py:20
  630.7 55.3 %collective-permute-start.9 = (bf16[128,1152]{1,0:T(8,128)(2,1)S(1)}, bf16[128,1152]{1,0:T(8,128)(2,1)S(1)}, u32[]{:S(2)}, u32[]{:S(2)}) collective-permute-start(bf16[128,1152]{1,0:T(8,128)(2,1)S(1)} %copy-done.123), channel_id=1, source_target_pairs={{2,0},{3,1},{4,2},{5,3},{6,4},{7,5},{8,6},{9,7},{10,8},{11,9},{12,... | collective-permute-start | bytes 884744 | tf_op jit(solution)/shard_map/ppermute | solution.py:20
  632.0 56.1 %collective-permute-start.10 = (bf16[128,1152]{1,0:T(8,128)(2,1)S(1)}, bf16[128,1152]{1,0:T(8,128)(2,1)S(1)}, u32[]{:S(2)}, u32[]{:S(2)}) collective-permute-start(bf16[128,1152]{1,0:T(8,128)(2,1)S(1)} %copy-done.123), channel_id=1, source_target_pairs={{3,0},{4,1},{5,2},{6,3},{7,4},{8,5},{9,6},{10,7},{11,8},{12,9},{13... | collective-permute-start | bytes 884744 | tf_op jit(solution)/shard_map/ppermute | solution.py:20
  709.6 64.3 %collective-permute-start.30 = (bf16[128,1152]{1,0:T(8,128)(2,1)}, bf16[128,1152]{1,0:T(8,128)(2,1)}, u32[]{:S(2)}, u32[]{:S(2)}) collective-permute-start(bf16[128,1152]{1,0:T(8,128)(2,1)} %convolution_convert_fusion.3), channel_id=1, source_target_pairs={{7,0},{8,1},{9,2},{10,3},{11,4},{12,5},{13,6},{14,7},{15,8},{16,9}... | collective-permute-start | bytes 884744 | tf_op jit(solution)/shard_map/ppermute | solution.py:20
  713.8 61.8 %collective-permute-start.31 = (bf16[128,1152]{1,0:T(8,128)(2,1)}, bf16[128,1152]{1,0:T(8,128)(2,1)}, u32[]{:S(2)}, u32[]{:S(2)}) collective-permute-start(bf16[128,1152]{1,0:T(8,128)(2,1)} %convolution_convert_fusion.3), channel_id=1, source_target_pairs={{8,0},{9,1},{10,2},{11,3},{12,4},{13,5},{14,6},{15,7},{16,8},{17,9... | collective-permute-start | bytes 884744 | tf_op jit(solution)/shard_map/ppermute | solution.py:20
  1073.1 93.6 %collective-permute-start.111 = (bf16[128,1152]{0,1:T(8,128)(2,1)}, bf16[128,1152]{0,1:T(8,128)(2,1)S(1)}, u32[]{:S(2)}, u32[]{:S(2)}) collective-permute-start(bf16[128,1152]{0,1:T(8,128)(2,1)} %bitcast.87), channel_id=1, source_target_pairs={{0,8},{1,9},{2,10},{3,11},{4,12},{5,13},{6,14},{7,15},{8,16},{9,17... | collective-permute-start | bytes 884744 | tf_op jit(solution)/shard_map/ppermute | solution.py:20
  1082.0 88.4 %collective-permute-start.110 = (bf16[128,1152]{0,1:T(8,128)(2,1)}, bf16[128,1152]{0,1:T(8,128)(2,1)}, u32[]{:S(2)}, u32[]{:S(2)}) collective-permute-start(bf16[128,1152]{0,1:T(8,128)(2,1)} %bitcast.86), channel_id=1, source_target_pairs={{0,7},{1,8},{2,9},{3,10},{4,11},{5,12},{6,13},{7,14},{8,15},{9,16}... | collective-permute-start | bytes 884744 | tf_op jit(solution)/shard_map/ppermute | solution.py:20
  1093.3 78.5 %collective-permute-start.109 = (bf16[128,1152]{0,1:T(8,128)(2,1)}, bf16[128,1152]{0,1:T(8,128)(2,1)}, u32[]{:S(2)}, u32[]{:S(2)}) collective-permute-start(bf16[128,1152]{0,1:T(8,128)(2,1)} %bitcast.85), channel_id=1, source_target_pairs={{0,6},{1,7},{2,8},{3,9},{4,10},{5,11},{6,12},{7,13},{8,14},{9,15},... | collective-permute-start | bytes 884744 | tf_op jit(solution)/shard_map/ppermute | solution.py:20
  1103.5 74.8 %collective-permute-start.108 = (bf16[128,1152]{0,1:T(8,128)(2,1)}, bf16[128,1152]{0,1:T(8,128)(2,1)}, u32[]{:S(2)}, u32[]{:S(2)}) collective-permute-start(bf16[128,1152]{0,1:T(8,128)(2,1)} %bitcast.84), channel_id=1, source_target_pairs={{0,5},{1,6},{2,7},{3,8},{4,9},{5,10},{6,11},{7,12},{8,13},{9,14},{... | collective-permute-start | bytes 884744 | tf_op jit(solution)/shard_map/ppermute | solution.py:20
  1128.5 51.2 %collective-permute-start.107 = (bf16[128,1152]{0,1:T(8,128)(2,1)}, bf16[128,1152]{0,1:T(8,128)(2,1)}, u32[]{:S(2)}, u32[]{:S(2)}) collective-permute-start(bf16[128,1152]{0,1:T(8,128)(2,1)} %bitcast.83), channel_id=1, source_target_pairs={{0,4},{1,5},{2,6},{3,7},{4,8},{5,9},{6,10},{7,11},{8,12},{9,13},{1... | collective-permute-start | bytes 884744 | tf_op jit(solution)/shard_map/ppermute | solution.py:20
  1293.7 49.2 %collective-permute-start.113 = (bf16[128,1152]{0,1:T(8,128)(2,1)}, bf16[128,1152]{0,1:T(8,128)(2,1)S(1)}, u32[]{:S(2)}, u32[]{:S(2)}) collective-permute-start(bf16[128,1152]{0,1:T(8,128)(2,1)} %bitcast.517), channel_id=1, source_target_pairs={{7,0},{8,1},{9,2},{10,3},{11,4},{12,5},{13,6},{14,7},{15,8},{16,9}... | collective-permute-start | bytes 884744 | tf_op jit(solution)/shard_map/ppermute | solution.py:20
  1299.1 46.6 %collective-permute-start.112 = (bf16[128,1152]{0,1:T(8,128)(2,1)}, bf16[128,1152]{0,1:T(8,128)(2,1)S(1)}, u32[]{:S(2)}, u32[]{:S(2)}) collective-permute-start(bf16[128,1152]{0,1:T(8,128)(2,1)} %bitcast.515), channel_id=1, source_target_pairs={{8,0},{9,1},{10,2},{11,3},{12,4},{13,5},{14,6},{15,7},{16,8},{17,9... | collective-permute-start | bytes 884744 | tf_op jit(solution)/shard_map/ppermute | solution.py:20
  1388.1 50.5 %collective-permute-start.65 = (bf16[128,1152]{0,1:T(8,128)(2,1)S(1)}, bf16[128,1152]{0,1:T(8,128)(2,1)S(1)}, u32[]{:S(2)}, u32[]{:S(2)}) collective-permute-start(bf16[128,1152]{0,1:T(8,128)(2,1)S(1)} %bitcast.502), channel_id=1, source_target_pairs={{7,0},{8,1},{9,2},{10,3},{11,4},{12,5},{13,6},{14,7},{15,8},{16,9}... | collective-permute-start | bytes 884744 | tf_op jit(solution)/shard_map/ppermute | solution.py:20
  1393.4 50.8 %collective-permute-start.64 = (bf16[128,1152]{0,1:T(8,128)(2,1)S(1)}, bf16[128,1152]{0,1:T(8,128)(2,1)S(1)}, u32[]{:S(2)}, u32[]{:S(2)}) collective-permute-start(bf16[128,1152]{0,1:T(8,128)(2,1)S(1)} %bitcast.500), channel_id=1, source_target_pairs={{8,0},{9,1},{10,2},{11,3},{12,4},{13,5},{14,6},{15,7},{16,8},{17,9... | collective-permute-start | bytes 884744 | tf_op jit(solution)/shard_map/ppermute | solution.py:20
  1414.0 47.1 %collective-permute-start.94 = (bf16[128,1152]{0,1:T(8,128)(2,1)S(1)}, bf16[128,1152]{0,1:T(8,128)(2,1)S(1)}, u32[]{:S(2)}, u32[]{:S(2)}) collective-permute-start(bf16[128,1152]{0,1:T(8,128)(2,1)S(1)} %bitcast.501), channel_id=1, source_target_pairs={{0,7},{1,8},{2,9},{3,10},{4,11},{5,12},{6,13},{7,14},{8,15},{9,16}... | collective-permute-start | bytes 884744 | tf_op jit(solution)/shard_map/ppermute | solution.py:20
  (293 other events, 10448.5 us)
Sparse Core Ops, SparseCore 0:
  11.2 73.1 all-gather.18
  87.5 93.6 all-gather.20
  184.4 67.4 all-gather.22
  254.9 67.4 all-gather.24
  325.6 153.1 all-gather.26
  481.9 182.1 all-gather.28
where the time goes:
time: 1950 us; the launch traced here: 1930 us
  waiting for transfers between devices  565 us (29%)
  starting transfers between devices  479 us (25%)
  blocking collectives  377 us (19%)
  matrix products  265 us (14%)
  local copies, waits for them, and re-layouts  149 us (8%)
  other arithmetic  75.7 us (4%)
    ppermute x128, starting transfers between devices, passed_along(): lax.ppermute(value, axis, [(source, source + steps) for source in range(f...  479 us
    psum x1, blocking collectives, body(): vectors = lax.psum(vec_sums, ('fsdp', 'rep'))  346 us
    ppermute x128, waiting for transfers between devices, passed_along(): lax.ppermute(value, axis, [(source, source + steps) for source in range(f...  302 us
    unnamed x458, local copies, waits for them, and re-layouts  76.9 us
    all_gather x1, waiting for transfers between devices, body(): lax.all_gather(shards[0], 'fsdp', axis=0, tiled=True)  72.4 us
    all_gather x1, waiting for transfers between devices, body(): lax.all_gather(shards[2], 'fsdp', axis=0, tiled=True)  67.6 us
    dot_general x12, matrix products, left_times(): lax.dot_general(left, right, (((0,), (0,)), ((), ())), preferred_element_...  64.3 us
    all_gather x1, waiting for transfers between devices, body(): lax.all_gather(shards[3], 'fsdp', axis=0, tiled=True)  59.9 us
  transfers between devices with their start and end apart: 134, of which 44 were waited for; matrix products, arithmetic and copies ran while one was open for 14% of the time, Pallas kernels for 0%

commit v1 on v0

v1 whole, which is shorter than its diff:
```python
import functools

import jax
import jax.numpy as jnp
import numpy as np
from jax import lax
from jax.experimental import pallas as pl
from jax.experimental.pallas import tpu as pltpu
from jax.sharding import PartitionSpec as P

MESH = pl.DeviceIdType.MESH
BF = jnp.bfloat16
F32 = jnp.float32
LANES = 128
ORDERS = (("x", "y", "z"), ("y", "z", "x"), ("z", "x", "y"))
AXES = ("x", "y", "z")


def here():
    shard = lax.axis_index("fsdp")
    low = lax.axis_index("rep")
    place = {
        "x": lax.div(shard, 16),
        "y": lax.rem(lax.div(shard, 8), 2) * 2 + low,
        "z": lax.rem(lax.div(shard, 2), 4),
    }
    return place, lax.rem(shard, 2)


def moved(place, axis, steps):
    steps = steps % 4
    if steps == 0:
        return place
    other = dict(place)
    other[axis] = lax.rem(place[axis] + steps, 4)
    return other


def device_at(place, core):
    high = lax.div(place["y"], 2)
    return (((place["x"] * 2 + high) * 4 + place["z"]) * 2 + core, lax.rem(place["y"], 2))


def greet(peers):
    barrier = pltpu.get_barrier_semaphore()
    for peer in peers:
        pl.semaphore_signal(barrier, inc=1, device_id=peer, device_id_type=MESH)
    pl.semaphore_wait(barrier, len(peers))


def torus_peers(place, core):
    peers = [device_at(place, 1 - core)]
    for axis in AXES:
        for steps in (1, 2, 3):
            peers.append(device_at(moved(place, axis, steps), core))
    return peers


def part_columns(part, half, width):
    return pl.ds(pl.multiple_of(part * 2 * width + half * width, LANES), width)


def piece_of(ref, part, width, place, core):
    return ref.at[
        place["x"],
        lax.div(place["y"], 2),
        place["z"],
        core,
        :,
        part_columns(part, lax.rem(place["y"], 2), width),
    ]


def block_of(ref, part, width, place, core, axis, half=None):
    where = {"x": place["x"], "y": lax.div(place["y"], 2), "z": place["z"]}
    if axis == "y":
        where["y"] = pl.ds(0, 2) if half is None else pl.ds(half, 1)
        columns = pl.ds(part * 2 * width, 2 * width)
    else:
        where[axis] = pl.ds(0, 4) if half is None else pl.ds(2 * half, 2)
        columns = part_columns(part, lax.rem(place["y"], 2), width)
    return ref.at[where["x"], where["y"], where["z"], core, :, columns]


GATHER_SEMS = 3 + 3 + 8 + 8 + 16


def gather_kernel(width, own, full, send, recv, local):
    place, core = here()
    greet(torus_peers(place, core))
    twin = device_at(place, 1 - core)
    started = []

    def sem_index(part, kind, index):
        return part * GATHER_SEMS + {"a": 0, "b": 3, "c": 6, "d": 14, "s": 22}[kind] + index

    def push(source, target, slot, device):
        copy = pltpu.make_async_remote_copy(
            src_ref=source,
            dst_ref=target,
            send_sem=send.at[slot],
            recv_sem=recv.at[slot],
            device_id=device,
            device_id_type=MESH,
        )
        copy.start()
        started.append(copy)

    def arrived(region, slot):
        pltpu.make_async_remote_copy(
            src_ref=region,
            dst_ref=region,
            send_sem=send.at[slot],
            recv_sem=recv.at[slot],
            device_id=twin,
            device_id_type=MESH,
        ).wait_recv()

    low = lax.rem(place["y"], 2)
    locals_ = []
    for part, (one, two, three) in enumerate(ORDERS):
        source = own.at[:, part_columns(part, low, width)]
        target = piece_of(full, part, width, place, core)
        copy = pltpu.make_async_copy(source, target, local.at[part])
        copy.start()
        locals_.append(copy)
        for steps in (1, 3, 2):
            push(
                source,
                target,
                sem_index(part, "a", steps - 1),
                device_at(moved(place, one, steps), core),
            )
    for part, (one, two, three) in enumerate(ORDERS):
        locals_[part].wait()
        for steps in (1, 3, 2):
            arrived(
                piece_of(full, part, width, moved(place, one, -steps), core),
                sem_index(part, "a", steps - 1),
            )
        block = block_of(full, part, width, place, core, one)
        for steps in (1, 3, 2):
            push(block, block, sem_index(part, "b", steps - 1), device_at(moved(place, two, steps), core))
        for way in (1, 3):
            push(block, block, sem_index(part, "c", (way // 2) * 4), device_at(moved(place, three, way), core))
        push(block, block, sem_index(part, "s", 0), twin)
    for steps in (1, 3, 2):
        for part, (one, two, three) in enumerate(ORDERS):
            block = block_of(full, part, width, moved(place, two, -steps), core, one)
            arrived(block, sem_index(part, "b", steps - 1))
            for way in (1, 3):
                push(
                    block,
                    block,
                    sem_index(part, "c", (way // 2) * 4 + steps),
                    device_at(moved(place, three, way), core),
                )
            push(block, block, sem_index(part, "s", steps), twin)
    for steps in (0, 1, 3, 2):
        for part, (one, two, three) in enumerate(ORDERS):
            for way in (1, 3):
                origin = moved(moved(place, two, -steps), three, -way)
                block = block_of(full, part, width, origin, core, one)
                arrived(block, sem_index(part, "c", (way // 2) * 4 + steps))
                piece = block_of(full, part, width, origin, core, one, way // 2)
                push(
                    piece,
                    piece,
                    sem_index(part, "d", (way // 2) * 4 + steps),
                    device_at(moved(place, three, way), core),
                )
                push(block, block, sem_index(part, "s", way * 4 + steps), twin)
    for steps in (0, 1, 3, 2):
        for part, (one, two, three) in enumerate(ORDERS):
            origin = moved(moved(place, two, -steps), three, 2)
            for way in (1, 3):
                arrived(
                    block_of(full, part, width, origin, core, one, way // 2),
                    sem_index(part, "d", (way // 2) * 4 + steps),
                )
            block = block_of(full, part, width, origin, core, one)
            push(block, block, sem_index(part, "s", 8 + steps), twin)
    for part, (one, two, three) in enumerate(ORDERS):
        for way in range(4):
            for steps in range(4):
                origin = moved(moved(place, two, -steps), three, -way)
                arrived(
                    block_of(full, part, width, origin, 1 - core, one),
                    sem_index(part, "s", way * 4 + steps),
                )
    for copy in started:
        copy.wait_send()


def gather_slab(slab, tag):
    total = slab.shape[1]
    width = total // 6
    full = pl.pallas_call(
        functools.partial(gather_kernel, width),
        out_shape=jax.ShapeDtypeStruct((4, 2, 4, 2, 16, total), slab.dtype),
        in_specs=[pl.BlockSpec(memory_space=pl.ANY)],
        out_specs=pl.BlockSpec(memory_space=pl.ANY),
        scratch_shapes=[
            pltpu.SemaphoreType.DMA((3 * GATHER_SEMS,)),
            pltpu.SemaphoreType.DMA((3 * GATHER_SEMS,)),
            pltpu.SemaphoreType.DMA((3,)),
        ],
        compiler_params=pltpu.CompilerParams(collective_id=tag, has_side_effects=True),
        name="gather_slab",
    )(slab)
    return full.reshape(1024, total)


def reduce_kernel(width, grads, out, *scratch):
    acc, sib, mid, far, side, line, done = [scratch[3 * i : 3 * i + 3] for i in range(7)]
    send, recv, local = scratch[21:]
    place, core = here()
    greet(torus_peers(place, core))
    twin = device_at(place, 1 - core)
    started = []
    count = 16 + 8 + 8 + 3 + 3 + 1

    def slot_of(part, kind, index):
        return part * count + {"s": 0, "m": 16, "f": 24, "d": 32, "l": 35, "o": 38}[kind] + index

    def push(source, target, slot, device):
        copy = pltpu.make_async_remote_copy(
            src_ref=source,
            dst_ref=target,
            send_sem=send.at[slot],
            recv_sem=recv.at[slot],
            device_id=device,
            device_id_type=MESH,
        )
        copy.start()
        started.append(copy)

    def arrived(region, slot):
        pltpu.make_async_remote_copy(
            src_ref=region,
            dst_ref=region,
            send_sem=send.at[slot],
            recv_sem=recv.at[slot],
            device_id=twin,
            device_id_type=MESH,
        ).wait_recv()

    def add(target, *terms):
        def row(index, carry):
            total = target[index].astype(F32)
            for term in terms:
                total = total + term[index].astype(F32)
            target[index] = total.astype(BF)
            return carry

        lax.fori_loop(0, target.shape[0], row, 0)

    def half_of(ref, half):
        size = ref.shape[0] // 2
        return ref.at[pl.ds(half * size, size)]

    loads = {}
    for ahead in (2, 1, 3, 0):
        for part, (one, two, three) in enumerate(ORDERS):
            for over in range(4):
                spot = moved(moved(place, two, over), three, ahead)
                push(
                    block_of(grads, part, width, spot, 1 - core, one),
                    sib[part].at[ahead, over],
                    slot_of(part, "s", ahead * 4 + over),
                    twin,
                )
                copy = pltpu.make_async_copy(
                    block_of(grads, part, width, spot, core, one),
                    acc[part].at[ahead, over],
                    local.at[part * 16 + ahead * 4 + over],
                )
                copy.start()
                loads[part, ahead, over] = copy

    def ready(part, ahead, over):
        loads[part, ahead, over].wait()
        arrived(sib[part].at[ahead, over], slot_of(part, "s", ahead * 4 + over))

    for over in range(4):
        for part, (one, two, three) in enumerate(ORDERS):
            ready(part, 2, over)
            add(acc[part].at[2, over], sib[part].at[2, over])
            for half, way in ((0, 3), (1, 1)):
                push(
                    half_of(acc[part].at[2, over], half),
                    mid[part].at[half, over],
                    slot_of(part, "m", half * 4 + over),
                    device_at(moved(place, three, way), core),
                )
    for over in range(4):
        for part, (one, two, three) in enumerate(ORDERS):
            for half, way in ((0, 3), (1, 1)):
                ready(part, way, over)
                add(acc[part].at[way, over], sib[part].at[way, over])
                arrived(mid[part].at[half, over], slot_of(part, "m", half * 4 + over))
                add(half_of(acc[part].at[way, over], half), mid[part].at[half, over])
                push(
                    acc[part].at[way, over],
                    far[part].at[half, over],
                    slot_of(part, "f", half * 4 + over),
                    device_at(moved(place, three, way), core),
                )
    for over in (2, 1, 3, 0):
        for part, (one, two, three) in enumerate(ORDERS):
            ready(part, 0, over)
            for half in range(2):
                arrived(far[part].at[half, over], slot_of(part, "f", half * 4 + over))
            add(
                acc[part].at[0, over],
                sib[part].at[0, over],
                far[part].at[0, over],
                far[part].at[1, over],
            )
            if over:
                push(
                    acc[part].at[0, over],
                    side[part].at[over - 1],
                    slot_of(part, "d", over - 1),
                    device_at(moved(place, two, over), core),
                )

    def piece(part, axis, spot):
        if axis == "y":
            return acc[part].at[
                0,
                0,
                lax.div(spot["y"], 2),
                :,
                pl.ds(pl.multiple_of(lax.rem(spot["y"], 2) * width, LANES), width),
            ]
        return acc[part].at[0, 0, spot[axis]]

    for part, (one, two, three) in enumerate(ORDERS):
        for over in (1, 2, 3):
            arrived(side[part].at[over - 1], slot_of(part, "d", over - 1))
        add(acc[part].at[0, 0], side[part].at[0], side[part].at[1], side[part].at[2])
        for over in (2, 1, 3):
            spot = moved(place, one, over)
            push(
                piece(part, one, spot),
                line[part].at[over - 1],
                slot_of(part, "l", over - 1),
                device_at(spot, core),
            )
    low = lax.rem(place["y"], 2)
    partner = (lax.axis_index("fsdp"), 1 - low)
    for part, (one, two, three) in enumerate(ORDERS):
        for over in (1, 2, 3):
            arrived(line[part].at[over - 1], slot_of(part, "l", over - 1))
        total = piece(part, one, place)[...].astype(F32)
        for over in range(3):
            total = total + line[part][over].astype(F32)
        done[part][...] = total.astype(BF)
        columns = part_columns(part, low, width)
        push(done[part], out.at[:, columns], slot_of(part, "o", 0), partner)
        out[:, columns] = done[part][...]
    for part in range(3):
        arrived(out.at[:, part_columns(part, 1 - low, width)], slot_of(part, "o", 0))
    for copy in started:
        copy.wait_send()


def reduce_slab(grads, tag):
    total = grads.shape[1]
    width = total // 6

    def shapes(lead, half=False):
        found = []
        for one, two, three in ORDERS:
            if one == "y":
                found.append(pltpu.VMEM(lead + (1 if half else 2, 16, 2 * width), BF))
            else:
                found.append(pltpu.VMEM(lead + (2 if half else 4, 16, width), BF))
        return found

    count = 16 + 8 + 8 + 3 + 3 + 1
    return pl.pallas_call(
        functools.partial(reduce_kernel, width),
        out_shape=jax.ShapeDtypeStruct((16, total), BF),
        in_specs=[pl.BlockSpec(memory_space=pl.ANY)],
        out_specs=pl.BlockSpec(memory_space=pltpu.VMEM),
        scratch_shapes=(
            shapes((4, 4))
            + shapes((4, 4))
            + shapes((2, 4), True)
            + shapes((2, 4))
            + shapes((3,))
            + [pltpu.VMEM((3, 16, width), BF)] * 3
            + [pltpu.VMEM((16, width), BF)] * 3
            + [
                pltpu.SemaphoreType.DMA((3 * count,)),
                pltpu.SemaphoreType.DMA((3 * count,)),
                pltpu.SemaphoreType.DMA((48,)),
            ]
        ),
        compiler_params=pltpu.CompilerParams(
            collective_id=tag, has_side_effects=True, vmem_limit_bytes=60 << 20
        ),
        name="reduce_slab",
    )(grads.reshape(4, 2, 4, 2, 16, total))


def swap_kernel(own, full, send, recv, local):
    place, core = here()
    low = lax.rem(place["y"], 2)
    mine = (place["z"] * 2 + core) * 2 + low
    base = lax.div(lax.axis_index("fsdp"), 8) * 8

    def peer(index):
        return (base + lax.div(index, 2), lax.rem(index, 2))

    def partner(k):
        zz = lax.rem(place["z"] + k // 4, 4)
        cc = lax.rem(core + (k // 2) % 2, 2)
        ll = lax.rem(low + k % 2, 2)
        return (zz * 2 + cc) * 2 + ll

    def source(k):
        zz = lax.rem(place["z"] + 4 - k // 4, 4)
        cc = lax.rem(core + (k // 2) % 2, 2)
        ll = lax.rem(low + k % 2, 2)
        return (zz * 2 + cc) * 2 + ll

    greet([peer(partner(k)) for k in range(1, 16)])
    keep = pltpu.make_async_copy(own.at[mine], full.at[mine], local.at[0])
    keep.start()
    copies = []
    for k in (9, 11, 5, 13, 7, 15, 1, 3, 8, 10, 4, 12, 6, 14, 2):
        target = partner(k)
        copy = pltpu.make_async_remote_copy(
            src_ref=own.at[target],
            dst_ref=full.at[mine],
            send_sem=send.at[k],
            recv_sem=recv.at[k],
            device_id=peer(target),
            device_id_type=MESH,
        )
        copy.start()
        copies.append(copy)
    for k in range(1, 16):
        region = full.at[source(k)]
        pltpu.make_async_remote_copy(
            src_ref=region,
            dst_ref=region,
            send_sem=send.at[k],
            recv_sem=recv.at[k],
            device_id=peer(partner(k)),
            device_id_type=MESH,
        ).wait_recv()
    keep.wait()
    for copy in copies:
        copy.wait_send()


def swap_heads(blocks, tag):
    return pl.pallas_call(
        swap_kernel,
        out_shape=jax.ShapeDtypeStruct(blocks.shape, blocks.dtype),
        in_specs=[pl.BlockSpec(memory_space=pl.ANY)],
        out_specs=pl.BlockSpec(memory_space=pl.ANY),
        scratch_shapes=[
            pltpu.SemaphoreType.DMA((16,)),
            pltpu.SemaphoreType.DMA((16,)),
            pltpu.SemaphoreType.DMA((1,)),
        ],
        compiler_params=pltpu.CompilerParams(collective_id=tag, has_side_effects=True),
        name="swap_heads",
    )(blocks)


D = 1152
HEADS = 16
HEAD_DIM = 72
FF = 4304
ROW = 2048
EPS = 1e-06
NEG = -1e30
SCALE = HEAD_DIM**-0.5
LEAD = 1024
TAIL = 128
PACK = 3 * HEAD_DIM
WIDE = 256
VALUE_LANE = 16
FF_PAD = 4352
STEP = 256
STEPS = FF_PAD // STEP
QKV = HEADS * PACK
ATTN_MAIN = QKV + D
ATTN_CHUNK = 640
ATTN_TOTAL = 5376
MLP_MAIN = 2 * FF_PAD
MLP_CHUNK = 1152
MLP_TOTAL = 9984
TANH_A = 0.7978845608028654
TANH_B = 0.044715


def dot(left, right):
    return jnp.dot(left, right, preferred_element_type=F32)


def dot_nt(left, right):
    return lax.dot_general(left, right, (((1,), (1,)), ((), ())), preferred_element_type=F32)


def dot_tn(left, right):
    return lax.dot_general(left, right, (((0,), (0,)), ((), ())), preferred_element_type=F32)


def origin(index):
    lead = (index >> 4) * 18 + (index & 15)
    rest = index - LEAD
    tail = (rest >> 1) * 18 + 16 + (rest & 1)
    return jnp.where(index < LEAD, lead, tail)


def iota(shape, axis):
    return lax.broadcasted_iota(jnp.int32, shape, axis)


def onehot(mask):
    return mask.astype(F32).astype(BF)


def pick_rows(chunk, count):
    return onehot(iota((TAIL, count), 1) == 8 * iota((TAIL, count), 0) + chunk)


def normal(values):
    center = values - jnp.mean(values, axis=-1, keepdims=True)
    rate = lax.rsqrt(jnp.mean(center * center, axis=-1, keepdims=True) + EPS)
    return center * rate, rate


def normal_back(unit, rate, gain, grad):
    inner = grad * gain
    first = jnp.mean(inner, axis=-1, keepdims=True)
    second = jnp.mean(inner * unit, axis=-1, keepdims=True)
    return rate * (inner - first - unit * second)


def column_total(values):
    return jnp.sum(values, axis=0, keepdims=True)


def lanes(start, size):
    return pl.ds(pl.multiple_of(start, LANES), size)


def params(limit=60):
    return pltpu.CompilerParams(vmem_limit_bytes=limit << 20)


def project_kernel(x_ref, weight_ref, vec_ref, bias_ref, heads_ref, h_ref, tail_ref, flat):
    unit, _ = normal(x_ref[...].astype(F32))
    h_ref[...] = (unit * vec_ref[0:1] + vec_ref[1:2]).astype(BF)

    def spread(chunk, carry):
        picked = dot(pick_rows(chunk, LEAD), weight_ref[:, ATTN_MAIN : ATTN_MAIN + ATTN_CHUNK])
        tail_ref[:, lanes(chunk * ATTN_CHUNK, ATTN_CHUNK)] = picked.astype(BF)
        return carry

    lax.fori_loop(0, 8, spread, 0)

    def columns(index, carry):
        place = lanes(index * 384, 384)
        value = dot(h_ref[:, :LEAD], weight_ref[:, place]) + dot(h_ref[:, LEAD:], tail_ref[:, place])
        flat[:, place] = (value + bias_ref[:, place]).astype(BF)
        return carry

    lax.fori_loop(0, QKV // 384, columns, 0)
    for head in range(HEADS):
        block = flat[:, PACK * head : PACK * head + PACK]
        heads_ref[head] = jnp.concatenate([block, jnp.zeros((256, WIDE - PACK), BF)], axis=1)


def project_heads(x, weight, vec, bias):
    return pl.pallas_call(
        project_kernel,
        out_shape=(
            jax.ShapeDtypeStruct((HEADS, 256, WIDE), BF),
            jax.ShapeDtypeStruct((256, D), BF),
            jax.ShapeDtypeStruct((TAIL, 8 * ATTN_CHUNK), BF),
        ),
        scratch_shapes=[pltpu.VMEM((256, QKV), BF)],
        compiler_params=params(),
        name="project_heads",
    )(x, weight, vec, bias)


def attend_kernel(spans, packed_ref, row_ref, col_ref, o_ref, keep_ref, keys, queries, scores):
    row = pl.program_id(0)
    packed = packed_ref[...].reshape(ROW, WIDE)
    lane = iota((ROW, LANES), 1)
    zero = jnp.zeros((ROW, LANES), BF)
    keys[...] = jnp.where(lane < HEAD_DIM, packed[:, :LANES], zero)
    turned = jnp.concatenate(
        [packed[:, HEAD_DIM : 2 * HEAD_DIM], jnp.zeros((ROW, LANES - HEAD_DIM), BF)], axis=1
    )
    queries[...] = turned

    def block(index, carry):
        rows = pl.ds(index * 256, 256)
        query = queries[rows, :]
        mine = col_ref[0, rows, :]
        low = spans[row * 16 + index]
        high = spans[row * 16 + 8 + index]

        def score(step, top):
            part = pl.ds(step * 256, 256)
            value = dot_nt(query, keys[part, :]) * SCALE
            value = jnp.where(mine == row_ref[0, :, lanes(step * 256, 256)], value, NEG)
            scores[:, lanes(step * 256, 256)] = value
            return jnp.maximum(top, jnp.maximum(value[:, :LANES], value[:, LANES:]))

        top = lax.fori_loop(low, high, score, jnp.full((256, LANES), NEG, F32))
        top = jnp.max(top, axis=1, keepdims=True)

        def weigh(step, carry):
            mass, total = carry
            expo = jnp.exp(scores[:, lanes(step * 256, 256)] - top)
            mass = mass + expo[:, :LANES] + expo[:, LANES:]
            value = packed_ref[pl.ds(step * 2, 2), :, LANES:].reshape(256, LANES)
            return mass, total + dot(expo.astype(BF), value)

        zeros = jnp.zeros((256, LANES), F32)
        mass, total = lax.fori_loop(low, high, weigh, (zeros, zeros))
        mass = jnp.sum(mass, axis=1, keepdims=True)
        total = total / mass
        o_ref[pl.ds(index * 2, 2)] = total.astype(BF).reshape(2, 128, LANES)
        lane = iota((256, LANES), 1)
        keep_ref[0, rows, :] = jnp.where(lane == 0, top + jnp.log(mass), total)
        return carry

    lax.fori_loop(0, 8, block, 0)


def attend(spans, packed, row_ids, col_ids):
    return pl.pallas_call(
        attend_kernel,
        out_shape=(
            jax.ShapeDtypeStruct((16, 256, LANES), BF),
            jax.ShapeDtypeStruct((2, ROW, LANES), F32),
        ),
        grid_spec=pltpu.PrefetchScalarGridSpec(
            num_scalar_prefetch=1,
            grid=(2,),
            in_specs=[
                pl.BlockSpec((16, 128, WIDE), lambda m, s: (0, m, 0)),
                pl.BlockSpec((1, 1, ROW), lambda m, s: (m, 0, 0)),
                pl.BlockSpec((1, ROW, 1), lambda m, s: (m, 0, 0)),
            ],
            out_specs=(
                pl.BlockSpec((16, 128, LANES), lambda m, s: (0, m, 0)),
                pl.BlockSpec((1, ROW, LANES), lambda m, s: (m, 0, 0)),
            ),
            scratch_shapes=[
                pltpu.VMEM((ROW, LANES), BF),
                pltpu.VMEM((ROW, LANES), BF),
                pltpu.VMEM((256, ROW), F32),
            ],
        ),
        compiler_params=params(),
        name="attend",
    )(spans, packed, row_ids, col_ids)


def attend_back_kernel(
    spans, packed_ref, go_ref, keep_ref, row_ref, col_ref, out_ref, keys, queries, dkeys, dvalues
):
    row = pl.program_id(0)
    packed = packed_ref[...].reshape(ROW, WIDE)
    lane = iota((ROW, LANES), 1)
    zero = jnp.zeros((ROW, LANES), BF)
    keys[...] = jnp.where(lane < HEAD_DIM, packed[:, :LANES], zero)
    turned = jnp.concatenate(
        [packed[:, HEAD_DIM : 2 * HEAD_DIM], jnp.zeros((ROW, LANES - HEAD_DIM), BF)], axis=1
    )
    queries[...] = turned
    dkeys[...] = jnp.zeros_like(dkeys)
    dvalues[...] = jnp.zeros_like(dvalues)

    def block(index, carry):
        rows = pl.ds(index * 256, 256)
        query = queries[rows, :]
        back = go_ref[pl.ds(index * 2, 2)].reshape(256, LANES)
        mine = row_ref[0, :, lanes(index * 256, 256)]
        low = spans[row * 16 + index]
        high = spans[row * 16 + 8 + index]
        kept = keep_ref[0, rows, :]
        inner = jnp.sum(back.astype(F32) * kept, axis=1, keepdims=True)
        lane = iota((256, LANES), 1)
        stats = jnp.transpose(jnp.where(lane == 0, kept, inner))
        logsum = stats[0:1]
        inner = stats[1:2]

        def step(part, total):
            span = pl.ds(part * 256, 256)
            key = keys[span, :]
            value = packed_ref[pl.ds(part * 2, 2), :, LANES:].reshape(256, LANES)
            score = dot_nt(key, query) * SCALE
            prob = jnp.exp(jnp.where(col_ref[0, span, :] == mine, score - logsum, NEG))
            grad = prob * (dot_nt(value, back) - inner)
            grad = grad.astype(BF)
            dvalues[span, :] += dot(prob.astype(BF), back)
            dkeys[span, :] += dot(grad, query)
            return total + dot_tn(grad, key)

        total = lax.fori_loop(low, high, step, jnp.zeros((256, LANES), F32)) * SCALE
        moved_q = jnp.concatenate(
            [
                jnp.zeros((256, HEAD_DIM), F32),
                total[:, :HEAD_DIM],
                jnp.zeros((256, WIDE - 2 * HEAD_DIM), F32),
            ],
            axis=1,
        )
        out_ref[pl.ds(index * 2, 2)] = moved_q.astype(BF).reshape(2, 128, WIDE)
        return carry

    lax.fori_loop(0, 8, block, 0)
    wide = jnp.concatenate([dkeys[...] * SCALE, dvalues[...]], axis=1)
    lane = iota((ROW, WIDE), 1)
    old = out_ref[...].reshape(ROW, WIDE)
    inside = (lane >= HEAD_DIM) & (lane < 2 * HEAD_DIM)
    out_ref[...] = jnp.where(inside, old, wide.astype(BF)).reshape(16, 128, WIDE)


def attend_back(spans, packed, go, keep, row_ids, col_ids):
    return pl.pallas_call(
        attend_back_kernel,
        out_shape=jax.ShapeDtypeStruct((16, 256, WIDE), BF),
        grid_spec=pltpu.PrefetchScalarGridSpec(
            num_scalar_prefetch=1,
            grid=(2,),
            in_specs=[
                pl.BlockSpec((16, 128, WIDE), lambda m, s: (0, m, 0)),
                pl.BlockSpec((16, 128, LANES), lambda m, s: (0, m, 0)),
                pl.BlockSpec((1, ROW, LANES), lambda m, s: (m, 0, 0)),
                pl.BlockSpec((1, 1, ROW), lambda m, s: (m, 0, 0)),
                pl.BlockSpec((1, ROW, 1), lambda m, s: (m, 0, 0)),
            ],
            out_specs=pl.BlockSpec((16, 128, WIDE), lambda m, s: (0, m, 0)),
            scratch_shapes=[
                pltpu.VMEM((ROW, LANES), BF),
                pltpu.VMEM((ROW, LANES), BF),
                pltpu.VMEM((ROW, LANES), F32),
                pltpu.VMEM((ROW, LANES), F32),
            ],
        ),
        compiler_params=params(),
        name="attend_back",
    )(spans, packed, go, keep, row_ids, col_ids)


def head_place(head):
    spot = iota((LANES, D), 0) - VALUE_LANE
    inside = (spot >= 0) & (spot < HEAD_DIM)
    return onehot(inside & (origin(iota((LANES, D), 1)) == HEAD_DIM * head + spot))


def unmix(value):
    return onehot(origin(iota((D, LANES), 0)) == value * LANES + iota((D, LANES), 1))


def middle_kernel(
    o_ref,
    x_ref,
    g_ref,
    out_a_ref,
    out_b_ref,
    vec_ref,
    bias_ref,
    up_ref,
    down_ref,
    whole_ref,
    mixed_ref,
    do_ref,
    dmid_ref,
    gout_ref,
    gvec_ref,
    gbias_ref,
    gw_ref,
    o_perm,
    mid,
    h2,
    h2_t,
    g_t,
    result,
    dh2,
    packed,
    tail,
    gtail,
    gup,
    gdown,
    gpack,
    sems,
):
    step = pl.program_id(0)

    @pl.when(step == 0)
    def _():
        fetch = pltpu.make_async_copy(
            whole_ref.at[:, pl.ds(MLP_MAIN, MLP_CHUNK)], packed, sems.at[4]
        )
        fetch.start()
        mid[...] = jnp.zeros_like(mid)

        def gather_head(head, carry):
            mid[...] += dot(o_ref[head], head_place(head))
            return carry

        lax.fori_loop(0, HEADS, gather_head, 0)
        o_perm[...] = mid[...].astype(BF)
        for part in range(3):
            place = slice(384 * part, 384 * part + 384)
            value = dot(o_perm[:, :LEAD], out_a_ref[:, place])
            value = value + dot(o_perm[:, LEAD:], out_b_ref[:, place])
            mid[:, place] = x_ref[:, place].astype(F32) + value + vec_ref[2:3, place]
        unit, _ = normal(mid[...])
        h2[...] = (unit * vec_ref[0:1] + vec_ref[1:2]).astype(BF)
        h2_t[...] = jnp.transpose(h2[...])
        g_t[...] = jnp.transpose(g_ref[...])
        result[...] = jnp.zeros_like(result)
        dh2[...] = jnp.zeros_like(dh2)
        gtail[:, MLP_MAIN:] = jnp.zeros((TAIL, 8 * MLP_CHUNK - MLP_MAIN), BF)
        fetch.wait()

        def spread(chunk, carry):
            picked = dot(pick_rows(chunk, LEAD), packed[...])
            tail[:, lanes(chunk * MLP_CHUNK, MLP_CHUNK)] = picked.astype(BF)
            return carry

        lax.fori_loop(0, 8, spread, 0)

    up_place = lanes(step * STEP, STEP)
    down_place = lanes(FF_PAD + step * STEP, STEP)
    up = up_ref[...]
    down = down_ref[...]
    up_tail = tail[:, up_place]
    down_tail = tail[:, down_place]
    pre = dot(h2[:, :LEAD], up) + dot(h2[:, LEAD:], up_tail) + bias_ref[...]
    square = pre * pre
    bend = jnp.tanh(TANH_A * pre * (1.0 + TANH_B * square))
    half = 0.5 * (1.0 + bend)
    active = (pre * half).astype(BF)
    slope = half + 0.5 * pre * (1.0 - bend * bend) * (TANH_A * (1.0 + 3.0 * TANH_B * square))
    back = dot(g_ref[:, :LEAD], down) + dot(g_ref[:, LEAD:], down_tail)
    dpre32 = back * slope
    dpre = dpre32.astype(BF)
    result[:, :LEAD] += dot_nt(active, down)
    result[:, LEAD:] += dot_nt(active, down_tail)
    dh2[:, :LEAD] += dot_nt(dpre, up)
    dh2[:, LEAD:] += dot_nt(dpre, up_tail)
    gbias_ref[...] = column_total(dpre.astype(F32))
    slot = lax.rem(step, 2)

    def leave(index, buffer, place):
        return pltpu.make_async_copy(
            buffer.at[slot], gw_ref.at[:, place], sems.at[index * 2 + slot]
        )

    @pl.when(step >= 2)
    def _():
        leave(0, gup, up_place).wait()
        leave(1, gdown, down_place).wait()

    gup[slot] = dot(h2_t[:LEAD], dpre).astype(BF)
    gdown[slot] = dot(g_t[:LEAD], active).astype(BF)
    leave(0, gup, up_place).start()
    leave(1, gdown, down_place).start()
    gtail[:, up_place] = dot(h2_t[LEAD:], dpre).astype(BF)
    gtail[:, down_place] = dot(g_t[LEAD:], active).astype(BF)

    @pl.when(step == STEPS - 1)
    def _():
        other = 1 - slot
        for index, buffer in ((0, gup), (1, gdown)):
            for which in (slot, other):
                pltpu.make_async_copy(
                    buffer.at[which], gw_ref.at[:, up_place], sems.at[index * 2 + which]
                ).wait()
        gpack[:, MLP_CHUNK:] = jnp.zeros((LEAD, LANES), BF)

        def collect(part, carry):
            total = jnp.zeros((LEAD, 384), F32)
            for chunk in range(8):
                place = lanes(chunk * MLP_CHUNK + part * 384, 384)
                total = total + dot_tn(pick_rows(chunk, LEAD), gtail[:, place])
            gpack[:, lanes(part * 384, 384)] = total.astype(BF)
            return carry

        lax.fori_loop(0, 3, collect, 0)
        leave_pack = pltpu.make_async_copy(
            gpack, gw_ref.at[:, pl.ds(MLP_MAIN, MLP_TOTAL - MLP_MAIN)], sems.at[4]
        )
        leave_pack.start()
        gain = vec_ref[0:1]
        unit, rate = normal(mid[...])
        grad = dh2[...]
        gvec_ref[...] = jnp.zeros_like(gvec_ref)
        gvec_ref[0:1] = column_total(grad * unit)
        gvec_ref[1:2] = column_total(grad)
        gvec_ref[3:4] = column_total(g_ref[...].astype(F32))
        dmid = g_ref[...].astype(F32) + normal_back(unit, rate, gain, grad)
        dmid_ref[...] = dmid
        dlow = dmid.astype(BF)
        gvec_ref[2:3] = column_total(dlow.astype(F32))
        mixed = (mid[...] + result[...] + vec_ref[3:4]).astype(BF)
        h2[...] = mixed

        def restore(index, carry):
            mixed_ref[:, lanes(index * LANES, LANES)] = dot(h2[...], unmix(index)).astype(BF)
            return carry

        lax.fori_loop(0, 9, restore, 0)
        g_t[...] = jnp.transpose(o_perm[...])
        h2[...] = dlow

        def outer(index, carry):
            rows = pl.ds(index * LANES, LANES)
            gout_ref[rows, :] = dot(g_t[rows, :], h2[...]).astype(BF)
            return carry

        lax.fori_loop(0, 9, outer, 0)
        o_perm[:, :LEAD] = dot_nt(h2[...], out_a_ref[...]).astype(BF)
        o_perm[:, LEAD:] = dot_nt(h2[...], out_b_ref[...]).astype(BF)

        def split_head(head, carry):
            do_ref[head] = dot_nt(o_perm[...], head_place(head)).astype(BF)
            return carry

        lax.fori_loop(0, HEADS, split_head, 0)
        leave_pack.wait()


def middle(o, x, g, attn, attn_tail, vec, bias, mlp):
    def whole(*shape):
        return pl.BlockSpec(shape, lambda i: (0,) * len(shape))

    return pl.pallas_call(
        middle_kernel,
        grid=(STEPS,),
        out_shape=(
            jax.ShapeDtypeStruct((256, D), BF),
            jax.ShapeDtypeStruct((HEADS, 256, LANES), BF),
            jax.ShapeDtypeStruct((256, D), F32),
            jax.ShapeDtypeStruct((D, D), BF),
            jax.ShapeDtypeStruct((8, D), F32),
            jax.ShapeDtypeStruct((1, FF_PAD), F32),
            jax.ShapeDtypeStruct((LEAD, MLP_TOTAL), BF),
        ),
        in_specs=[
            whole(HEADS, 256, LANES),
            whole(256, D),
            whole(256, D),
            pl.BlockSpec((LEAD, D), lambda i: (0, 3)),
            pl.BlockSpec((TAIL, D), lambda i: (0, 3)),
            whole(8, D),
            pl.BlockSpec((1, STEP), lambda i: (0, i)),
            pl.BlockSpec((LEAD, STEP), lambda i: (0, i)),
            pl.BlockSpec((LEAD, STEP), lambda i: (0, STEPS + i)),
            pl.BlockSpec(memory_space=pl.ANY),
        ],
        out_specs=(
            whole(256, D),
            whole(HEADS, 256, LANES),
            whole(256, D),
            whole(D, D),
            whole(8, D),
            pl.BlockSpec((1, STEP), lambda i: (0, i)),
            pl.BlockSpec(memory_space=pl.ANY),
        ),
        scratch_shapes=[
            pltpu.VMEM((256, D), BF),
            pltpu.VMEM((256, D), F32),
            pltpu.VMEM((256, D), BF),
            pltpu.VMEM((D, 256), BF),
            pltpu.VMEM((D, 256), BF),
            pltpu.VMEM((256, D), F32),
            pltpu.VMEM((256, D), F32),
            pltpu.VMEM((LEAD, MLP_CHUNK), BF),
            pltpu.VMEM((TAIL, 8 * MLP_CHUNK), BF),
            pltpu.VMEM((TAIL, 8 * MLP_CHUNK), BF),
            pltpu.VMEM((2, LEAD, STEP), BF),
            pltpu.VMEM((2, LEAD, STEP), BF),
            pltpu.VMEM((LEAD, MLP_TOTAL - MLP_MAIN), BF),
            pltpu.SemaphoreType.DMA((5,)),
        ],
        compiler_params=params(),
        name="middle",
    )(o, x, g, attn, attn_tail, vec, bias, mlp, mlp, mlp)


def finish_kernel(
    dheads_ref,
    weight_ref,
    tail_ref,
    h_ref,
    x_ref,
    dmid_ref,
    gout_ref,
    vec_ref,
    tokens_ref,
    gvec_ref,
    gbias_ref,
    gw_ref,
    flat,
    h_t,
    gtail,
    dh,
):
    for head in range(HEADS):
        flat[:, PACK * head : PACK * head + PACK] = dheads_ref[head, :, :PACK]
    h_t[...] = jnp.transpose(h_ref[...])
    dh[...] = jnp.zeros_like(dh)
    gtail[:, QKV:ATTN_MAIN] = gout_ref[LEAD:, :]
    gtail[:, ATTN_MAIN:] = jnp.zeros((TAIL, 8 * ATTN_CHUNK - ATTN_MAIN), BF)
    gw_ref[:, QKV:ATTN_MAIN] = gout_ref[:LEAD, :]
    gw_ref[:, ATTN_MAIN + ATTN_CHUNK :] = jnp.zeros(
        (LEAD, ATTN_TOTAL - ATTN_MAIN - ATTN_CHUNK), BF
    )

    def columns(index, carry):
        place = lanes(index * 384, 384)
        value = flat[:, place]
        gbias_ref[:, place] = column_total(value.astype(F32))
        dh[:, :LEAD] += dot_nt(value, weight_ref[:, place])
        dh[:, LEAD:] += dot_nt(value, tail_ref[:, place])
        gw_ref[:, place] = dot(h_t[:LEAD], value).astype(BF)
        gtail[:, place] = dot(h_t[LEAD:], value).astype(BF)
        return carry

    lax.fori_loop(0, QKV // 384, columns, 0)

    def collect(part, carry):
        total = jnp.zeros((LEAD, LANES), F32)
        for chunk in range(8):
            place = lanes(chunk * ATTN_CHUNK + part * LANES, LANES)
            total = total + dot_tn(pick_rows(chunk, LEAD), gtail[:, place])
        gw_ref[:, lanes(ATTN_MAIN + part * LANES, LANES)] = total.astype(BF)
        return carry

    lax.fori_loop(0, ATTN_CHUNK // LANES, collect, 0)
    unit, rate = normal(x_ref[...].astype(F32))
    grad = dh[...]
    gvec_ref[...] = jnp.zeros_like(gvec_ref)
    gvec_ref[0:1] = column_total(grad * unit)
    gvec_ref[1:2] = column_total(grad)
    total = dmid_ref[...] + normal_back(unit, rate, vec_ref[0:1], grad)
    flat[:, :D] = total.astype(BF)

    def restore(index, carry):
        tokens_ref[:, lanes(index * LANES, LANES)] = dot(flat[:, :D], unmix(index)).astype(BF)
        return carry

    lax.fori_loop(0, 9, restore, 0)


def finish(dheads, weight, tail, h, x, dmid, gout, vec):
    return pl.pallas_call(
        finish_kernel,
        out_shape=(
            jax.ShapeDtypeStruct((256, D), BF),
            jax.ShapeDtypeStruct((8, D), F32),
            jax.ShapeDtypeStruct((1, QKV), F32),
            jax.ShapeDtypeStruct((LEAD, ATTN_TOTAL), BF),
        ),
        scratch_shapes=[
            pltpu.VMEM((256, QKV), BF),
            pltpu.VMEM((D, 256), BF),
            pltpu.VMEM((TAIL, 8 * ATTN_CHUNK), BF),
            pltpu.VMEM((256, D), F32),
        ],
        compiler_params=params(),
        name="finish",
    )(dheads, weight, tail, h, x, dmid, gout, vec)


def pack_slab(weight, chunk, total):
    width = weight.shape[1]
    rest = jnp.pad(weight[16:], ((0, 0), (0, 8 * chunk - width))).reshape(16, chunk)
    return jnp.concatenate(
        [weight[:16], rest, jnp.zeros((16, total - width - chunk), weight.dtype)], axis=1
    )


def unpack_slab(slab, width, chunk):
    rest = slab[:, width : width + chunk].reshape(2, 8 * chunk)[:, :width]
    return jnp.concatenate([slab[:, :width], rest], axis=0).astype(F32)


def by_head(key, query, value):
    rows = key.shape[0]
    parts = [item.reshape(rows, HEADS, 1, HEAD_DIM) for item in (key, query, value)]
    return jnp.concatenate(parts, axis=2).reshape(rows, QKV)


def from_heads(value):
    parts = value.reshape(value.shape[0], HEADS, 3, HEAD_DIM)
    return [parts[:, :, i].reshape(value.shape[0], D) for i in range(3)]


def mixing():
    return onehot(iota((D, D), 0) == origin(iota((D, D), 1)))


def mix_exact(value, back=False):
    matrix = mixing().astype(F32)
    if back:
        matrix = matrix.T
    return jnp.dot(value, matrix, precision=lax.Precision.HIGHEST)


def body(
    tokens,
    picture,
    cotangent,
    ln1_gain,
    ln1_bias,
    w_query,
    b_query,
    w_key,
    w_value,
    b_value,
    w_out,
    b_out,
    ln2_gain,
    ln2_bias,
    w_fc1,
    b_fc1,
    w_fc2,
    b_fc2,
):
    mix = mixing()
    out_cols = dot(w_out, mix).astype(BF)
    attn_slab = pack_slab(
        jnp.concatenate([by_head(w_key, w_query, w_value), out_cols], axis=1),
        ATTN_CHUNK,
        ATTN_TOTAL,
    )
    gap = ((0, 0), (0, FF_PAD - FF))
    mlp_slab = pack_slab(
        jnp.concatenate([jnp.pad(w_fc1, gap), jnp.pad(w_fc2.T, gap)], axis=1),
        MLP_CHUNK,
        MLP_TOTAL,
    )
    attn = gather_slab(attn_slab, 0)
    mlp = gather_slab(mlp_slab, 1)

    both = jnp.concatenate([tokens.reshape(256, D), cotangent.reshape(256, D)], axis=0)
    both = dot(both, mix).astype(BF)
    x, g = both[:256], both[256:]
    vec = mix_exact(jnp.stack([ln1_gain, ln1_bias, ln2_gain, ln2_bias, b_out, b_fc2]))
    vec1 = jnp.pad(vec[:2], ((0, 6), (0, 0)))
    vec2 = jnp.pad(vec[2:], ((0, 4), (0, 0)))
    bias = by_head(jnp.zeros((1, D), F32), b_query[None], b_value[None])

    group = lax.div(lax.axis_index("fsdp"), 8)
    ids = lax.dynamic_slice(picture, (0, group * ROW), (2, ROW))
    first = ids[:, 0::256]
    last = ids[:, 255::256]
    spot = jnp.arange(ROW, dtype=jnp.int32)[None, None, :]
    begin = jnp.min(jnp.where(ids[:, None, :] == first[:, :, None], spot, ROW), axis=2) // 256
    end = jnp.max(jnp.where(ids[:, None, :] == last[:, :, None], spot, -1), axis=2) // 256 + 1
    spans = jnp.concatenate([begin, end], axis=1).reshape(32).astype(jnp.int32)
    row_ids = ids[:, None, :]
    col_ids = ids[:, :, None]

    heads, h1, attn_tail = project_heads(x, attn, vec1, bias)
    packed = swap_heads(heads, 2)
    o, keep = attend(spans, packed, row_ids, col_ids)
    o = swap_heads(o, 3)
    mixed, go, dmid, gout, gvec2, gbias1, gmlp = middle(
        o, x, g, attn, attn_tail, vec2, jnp.pad(b_fc1, (0, FF_PAD - FF))[None], mlp
    )
    go = swap_heads(go, 4)
    dheads = attend_back(spans, packed, go, keep, row_ids, col_ids)
    dheads = swap_heads(dheads, 5)
    gtokens, gvec1, gbias, gattn = finish(dheads, attn, attn_tail, h1, x, dmid, gout, vec1)
    mlp_share = unpack_slab(reduce_slab(gmlp, 6), MLP_MAIN, MLP_CHUNK)
    attn_share = unpack_slab(reduce_slab(gattn, 7), ATTN_MAIN, ATTN_CHUNK)
    vectors, gbias, gbias1 = lax.psum(
        (jnp.concatenate([gvec1[:2], gvec2[:4]]), gbias, gbias1), ("fsdp", "rep")
    )
    vectors = mix_exact(vectors, True)
    grad_key, grad_query, grad_value = from_heads(attn_share[:, :QKV])
    _, bias_query, bias_value = from_heads(gbias)
    grad_out = mix_exact(attn_share[:, QKV:], True)
    grad_up = mlp_share[:, :FF]
    grad_down = mlp_share[:, FF_PAD : FF_PAD + FF].T
    return (
        mixed.reshape(2, 128, D),
        gtokens.reshape(2, 128, D),
        vectors[0],
        vectors[1],
        grad_query,
        bias_query[0],
        grad_key,
        grad_value,
        bias_value[0],
        grad_out,
        vectors[4],
        vectors[2],
        vectors[3],
        grad_up,
        gbias1[0, :FF],
        grad_down,
        vectors[5],
    )


def solution(mesh):
    placed = (
        P(None, ("fsdp", "rep"), None),
        P(),
        P(None, ("fsdp", "rep"), None),
        P(),
        P(),
        P("fsdp", None),
        P(),
        P("fsdp", None),
        P("fsdp", None),
        P(),
        P("fsdp", None),
        P(),
        P(),
        P(),
        P("fsdp", None),
        P(),
        P(None, "fsdp"),
        P(),
    )
    return jax.shard_map(
        body,
        mesh=mesh,
        in_specs=placed,
        out_specs=(
            P(None, ("fsdp", "rep"), None),
            P(None, ("fsdp", "rep"), None),
            P(),
            P(),
            P("fsdp", None),
            P(),
            P("fsdp", None),
            P("fsdp", None),
            P(),
            P("fsdp", None),
            P(),
            P(),
            P(),
            P("fsdp", None),
            P(),
            P(None, "fsdp"),
            P(),
        ),
        check_vma=False,
    )
```

time: 1950 us -> 576 us (0.30)
  waiting for transfers between devices: 565 us -> 0 us
  starting transfers between devices: 479 us -> 0 us
  Pallas kernels: 0 us -> 461 us
  blocking collectives: 377 us -> 67.7 us
  matrix products: 265 us -> 7.38 us
  local copies, waits for them, and re-layouts: 149 us -> 27.5 us
  other arithmetic: 75.7 us -> 3.37 us
    ppermute x128 -> x0, starting transfers between devices: 479 us -> none  [passed_along(): lax.ppermute(value, axis, [(source, source + steps) for source in range(f...]
    pallas_call x0 -> x13, Pallas kernels: none -> 461 us  [the longest x2 94.8 us: reduce_slab(): pl.pallas_call(functools.partial(reduce_kernel, width), out_shape=jax.Sha...]
    ppermute x128 -> x0, waiting for transfers between devices: 302 us -> none  [passed_along(): lax.ppermute(value, axis, [(source, source + steps) for source in range(f...]
    psum x1, blocking collectives: 346 us -> 67.7 us  [body(): lax.psum((jnp.concatenate([gvec1[:2], gvec2[:4]]), gbias, gbias1), ('fsdp...]
    all_gather x6 -> x0, waiting for transfers between devices: 259 us -> none  [the longest x1 72.4 us: body(): lax.all_gather(shards[0], 'fsdp', axis=0, tiled=True)]
    dot_general x48 -> x5, matrix products: 265 us -> 7.38 us  [the longest x3 5.06 us: mix_exact(): return jnp.dot(value, matrix, precision=lax.Precision.HIGHEST)]
    unnamed x458 -> x24, local copies, waits for them, and re-layouts: 76.9 us -> 0.39 us
    concatenate x8 -> x1, local copies, waits for them, and re-layouts: 35.4 us -> 0.01 us  [by_head(): return jnp.concatenate(parts, axis=2).reshape(rows, QKV)]
  transfers between devices with their start and end apart: 134 -> 0, of which waited for: 44 -> 0; matrix products, arithmetic and copies ran while one was open for 14% -> 0% of each run, Pallas kernels for 0% -> 0%
where the time goes in v1:
time: 576 us; the launch traced here: 569 us
  Pallas kernels  461 us (80%)
  blocking collectives  67.7 us (12%)
  local copies, waits for them, and re-layouts  27.5 us (5%)
  matrix products  7.38 us (1%)
    pallas_call x2, Pallas kernels, reduce_slab(): pl.pallas_call(functools.partial(reduce_kernel, width), out_shape=jax.Sha...  94.8 us
    pallas_call x2, Pallas kernels, gather_slab(): pl.pallas_call(functools.partial(gather_kernel, width), out_shape=jax.Sha...  90.3 us
    pallas_call x4, Pallas kernels, swap_heads(): pl.pallas_call(swap_kernel, out_shape=jax.ShapeDtypeStruct(blocks.shape,...  89.2 us
    psum x1, blocking collectives, body(): lax.psum((jnp.concatenate([gvec1[:2], gvec2[:4]]), gbias, gbias1), ('fsdp...  67.7 us
    pallas_call x1, Pallas kernels, middle(): pl.pallas_call(middle_kernel, grid=(STEPS,), out_shape=(jax.ShapeDtypeStr...  62.6 us
    pallas_call x1, Pallas kernels, attend_back(): pl.pallas_call(attend_back_kernel, out_shape=jax.ShapeDtypeStruct((16, 25...  45.3 us
    pallas_call x1, Pallas kernels, attend(): pl.pallas_call(attend_kernel, out_shape=(jax.ShapeDtypeStruct((16, 256, L...  37.8 us
    pallas_call x1, Pallas kernels, finish(): pl.pallas_call(finish_kernel, out_shape=(jax.ShapeDtypeStruct((256, D), B...  26.9 us

profile of v1, /device:TPU:0, one launch (start us, length us, event | category | flops | bytes accessed | tf_op | source)
XLA Modules:
  0.0 568.6 jit_solution(11484031012240182559)
XLA Ops:
  5.0 0.8 reshape_broadcast_in_dim.6
  5.8 0.8 reshape_broadcast_in_dim.7
  9.2 1.3 fusion.2
  16.8 1.9 fusion.5
  18.6 1.1 fusion.46
  19.7 2.0 copy.46.col_ref
  21.7 37.9 %gather_slab.2 = bf16[4,2,4,2,16,5376]{5,4,3,2,1,0:T(8,128)(2,1)} custom-call(bf16[16,5376]{1,0:T(8,128)(2,1)} %pad_maximum_fusion.2.own), custom_call_target="tpu_custom_call" | custom-call | tf_op jit(solution)/shard_map/gather_slab/pallas_call | solution.py:198
  59.6 14.3 %project_heads.1 = (bf16[16,256,256]{2,1,0:T(8,128)(2,1)}, bf16[256,1152]{1,0:T(8,128)(2,1)}, bf16[128,5120]{1,0:T(8,128)(2,1)}) custom-call(bf16[256,1152]{1,0:T(8,128)(2,1)} %get-tuple-element.66.x_ref, bf16[1024,5376]{1,0:T(8,128)(2,1)} %bitcast.22, f32[8,1152]{1,0:T(8,128)} %pad.28.vec_ref, f32[1,3456]{1,0:T(1,128)} %reshape.113.bias_ref), custom_call_target="tpu_custom_call" | custom-call | tf_op jit(solution)/shard_map/project_heads/pallas_call | solution.py:584
  73.9 27.3 %swap_heads.4.packed_ref = bf16[16,256,256]{2,1,0:T(8,128)(2,1)} custom-call(bf16[16,256,256]{2,1,0:T(8,128)(2,1)} %get-tuple-element.33.own), custom_call_target="tpu_custom_call" | custom-call | tf_op jit(solution)/shard_map/swap_heads/pallas_call | solution.py:462
  101.2 37.8 %attend.1 = (bf16[16,256,128]{2,1,0:T(8,128)(2,1)}, f32[2,2048,128]{2,1,0:T(8,128)}) custom-call(s32[32]{0:T(128)} %reshape.103.spans, bf16[16,256,256]{2,1,0:T(8,128)(2,1)} %swap_heads.4.packed_ref, s32[2,1,2048]{2,1,0:T(1,128)} %broadcast_in_dim.38.row_ref, s32[2,2048,1]{2,1,0:T(8,128)} %copy.46.col_ref), custom_call_target="tpu_custom_call" | custom-call | tf_op jit(solution)/shard_map/attend/pallas_call | solution.py:645
  139.0 16.8 %swap_heads.5.o_ref = bf16[16,256,128]{2,1,0:T(8,128)(2,1)} custom-call(bf16[16,256,128]{2,1,0:T(8,128)(2,1)} %get-tuple-element.34.own), custom_call_target="tpu_custom_call" | custom-call | tf_op jit(solution)/shard_map/swap_heads/pallas_call | solution.py:462
  155.9 52.4 %gather_slab.3 = bf16[4,2,4,2,16,9984]{5,4,3,2,1,0:T(8,128)(2,1)} custom-call(bf16[16,9984]{1,0:T(8,128)(2,1)} %pad_maximum_fusion.own), custom_call_target="tpu_custom_call" | custom-call | tf_op jit(solution)/shard_map/gather_slab/pallas_call | solution.py:198
  208.3 62.6 %middle.1 = (bf16[256,1152]{1,0:T(8,128)(2,1)}, bf16[16,256,128]{2,1,0:T(8,128)(2,1)}, f32[256,1152]{1,0:T(8,128)}, bf16[1152,1152]{1,0:T(8,128)(2,1)}, f32[8,11...) custom-call(bf16[16,256,128]{2,1,0:T(8,128)(2,1)} %swap_heads.5.o_ref, ...), custom_call_target="tpu_custom_call" | custom-call | tf_op jit(solution)/shard_map/middle/pallas_call | solution.py:947
  270.8 0.8 slice.114
  271.6 57.6 %reduce_slab.3 = bf16[16,9984]{1,0:T(8,128)(2,1)} custom-call(bf16[4,2,4,2,16,9984]{5,4,3,2,1,0:T(8,128)(2,1)} %bitcast.25), custom_call_target="tpu_custom_call" | custom-call | tf_op jit(solution)/shard_map/reduce_slab/pallas_call | solution.py:383
  329.3 0.8 slice.131
  330.0 1.0 slice.130
  331.1 0.9 slice_bitcast_fusion
  332.1 17.1 %swap_heads.6.go_ref = bf16[16,256,128]{2,1,0:T(8,128)(2,1)} custom-call(bf16[16,256,128]{2,1,0:T(8,128)(2,1)} %get-tuple-element.37.own), custom_call_target="tpu_custom_call" | custom-call | tf_op jit(solution)/shard_map/swap_heads/pallas_call | solution.py:462
  349.2 45.3 %attend_back.1.own = bf16[16,256,256]{2,1,0:T(8,128)(2,1)} custom-call(s32[32]{0:T(128)} %reshape.103.spans, bf16[16,256,256]{2,1,0:T(8,128)(2,1)} %swap_heads.4.packed_ref, bf16[16,256,128]{2,1,0:T(8,128)(2,1)} %swap_heads.6.go_ref, f32[2,2048,128]{2,1,0:T(8,128)} %get-tuple-element.38.keep_ref, s32[2,1,2048]{2,1,0:T(1,128)} %broadcast_in_dim.38.row_ref, ...), custom_call_target="tpu_custom_call" | custom-call | tf_op jit(solution)/shard_map/attend_back/pallas_call | solution.py:736
  394.5 28.0 %swap_heads.7.dheads_ref = bf16[16,256,256]{2,1,0:T(8,128)(2,1)} custom-call(bf16[16,256,256]{2,1,0:T(8,128)(2,1)} %attend_back.1.own), custom_call_target="tpu_custom_call" | custom-call | tf_op jit(solution)/shard_map/swap_heads/pallas_call | solution.py:462
  422.5 26.9 %finish.1 = (bf16[256,1152]{1,0:T(8,128)(2,1)}, f32[8,1152]{1,0:T(8,128)}, f32[1,3456]{1,0:T(1,128)}, bf16[1024,5376]{1,0:T(8,128)(2,1)}) custom-call(bf16[16,256,256]{2,1,0:T(8,128)(2,1)} %swap_heads.7.dheads_ref, bf16[1024,5376]{1,0:T(8,128)(2,1)} %bitcast.24, bf16[128,5120]{1,0:T(8,128)(2,1)} %get-tuple-element.35.out_b_ref.tail_ref, ...), custom_call_target="tpu_custom_call" | custom-call | tf_op jit(solution)/shard_map/finish/pallas_call | solution.py:1067
  449.4 0.8 slice.113
  451.1 67.7 %all-reduce.7 = (f32[6,1152]{1,0:T(8,128)S(1)}, f32[1,16,3,72]{3,2,1,0:T(4,128)S(1)}, f32[1,4352]{1,0:T(1,128)S(1)}) all-reduce(f32[6,1152]{1,0:T(8,128)S(1)} %pad_maximum_fusion.5, f32[1,16,3,72]{3,2,1,0:T(4,128)S(1)} %reshape.122, f32[1,4352]{1,0:T(1,128)S(1)} %copy-done.8), channel_id=1, replica_groups=mesh['fsdp'=64,'rep'=2] {'fsdp','rep'}, use_global_device_ids=true, to_apply=%region_2.3 | all-reduce | flops 14720 | bytes 117760 | tf_op jit(solution)/shard_map/psum | solution.py:1189
  518.7 2.2 fusion.1
  523.7 37.1 %reduce_slab.2 = bf16[16,5376]{1,0:T(8,128)(2,1)} custom-call(bf16[4,2,4,2,16,5376]{5,4,3,2,1,0:T(8,128)(2,1)} %bitcast.26), custom_call_target="tpu_custom_call" | custom-call | tf_op jit(solution)/shard_map/reduce_slab/pallas_call | solution.py:383
  561.6 0.9 slice.117
  562.5 1.5 fusion
  564.6 1.2 slice_reduce_fusion
  565.8 0.8 reshape_squeeze.11
  566.6 0.8 reshape_squeeze.10
  567.4 0.8 reshape_squeeze.9
  (84 shorter events, 18.0 us)
Async XLA Ops:
  0.7 6.7 %copy-start = (s32[2,16384]{1,0:T(2,128)S(1)}, s32[2,16384]{1,0:T(2,128)}, u32[]{:S(2)}) copy-start(s32[2,16384]{1,0:T(2,128)} %param.19) | copy-start | bytes 393220
  0.7 10.5 %copy-start.7 = (f32[4304]{0:T(1024)S(1)}, f32[4304]{0:T(1024)}, u32[]{:S(2)}) copy-start(f32[4304]{0:T(1024)} %param.33) | copy-start | bytes 51652
  0.7 11.7 %copy-start.11 = (bf16[18,1152]{1,0:T(8,128)(2,1)S(1)}, bf16[18,1152]{1,0:T(8,128)(2,1)}, u32[]{:S(2)}) copy-start(bf16[18,1152]{1,0:T(8,128)(2,1)} %param.28) | copy-start | bytes 124420
  12.4 0.8 copy-start.4
  12.4 1.1 copy-start.5
  12.4 1.4 copy-start.6
  13.2 2.6 copy-start.2
  13.2 2.6 copy-start.3
  13.2 3.5 copy-start.9
  13.2 3.5 copy-start.10
  422.5 28.5 %copy-start.8 = (f32[1,4352]{1,0:T(1,128)S(1)}, f32[1,4352]{1,0:T(1,128)}, u32[]{:S(2)}) copy-start(f32[1,4352]{1,0:T(1,128)} %get-tuple-element.48) | copy-start | bytes 52228
  562.5 5.7 copy-start.1
